TPU v7x, 32 devices: a whole 2x2x4 slice. The times are simulated.
32 devices in a mesh: blk: 16 (over z, x, core), help: 2 (over y).
Axes of the slice: x: 2, y: 2, z: 4, core: 2. Of those that a mesh axis runs over, the one named last changes fastest.
Arguments:
- features_t: bfloat16 [256, 24576], P(None, 'blk'), may hold values from -6 to 6
- weight: bfloat16 [256, 256], replicated, may hold values from -0.375 to 0.375
- bias: float32 [256], P('help'), may hold values from -3 to 3
- cotangent_t: bfloat16 [256, 24576], P('help', 'blk'), may hold values from -6 to 6
- tile_vals: bfloat16 [16, 2, 80, 128, 128], P('blk', 'help'), may hold values from -0.15625 to 0.15625
- slot_row: int32 [16, 2, 80], P('blk', 'help'), may hold values from 0 to 12, as said below
- slot_col: int32 [16, 2, 80], P('blk', 'help'), may hold values from 0 to 59, as said below
Outputs:
- output_t: bfloat16 [256, 24576], P('help', 'blk')
- propagated_grad: float32 [256, 24576], P('help', 'blk')
- weight_grad: float32 [256, 256], P(None, 'help')
- bias_grad: float32 [256], P('help')
Inputs may be any that keep to these rules, and one draw needn't show every extreme that they name: `slot_row`: each device has 80 slots, the used ones first; a slot holding 12 is unused. In every node-row block one helper uses all 80 slots and every other one at least 40. A slot's column tile is tile slot_col % 12 of node-row block (own block + slot_col // 12 - 2) taken around the loop of 16 blocks.
All inputs are finite; a program needn't handle non-finite values.
Results may differ from a plain program's by a relative error of at most 0.0045.
Values may be sent and summed in bfloat16 or wider, within the bound.
A program may use at most 64 MiB of HBM per device.

v0:
```python
import math

import jax
import jax.numpy as jnp
from jax import lax
from jax.sharding import PartitionSpec as P

BAND = 2


def shifted(block, axis, distance):
    devices = range(lax.axis_size(axis))
    route = [((i - distance) % len(devices), i) for i in devices]
    return lax.ppermute(block, axis, route)


def gather_window(block):
    placed = []
    for offset in range(-BAND, BAND + 1):
        if offset == 0:
            placed.append(block)
        else:
            placed.append(shifted(block, "blk", -offset))
    stacked = jnp.stack(placed, axis=0)
    return stacked


def aggregate(stacked, tiles, rows, cols, row_tiles):
    tile = tiles.shape[-1]
    spans = stacked.shape[0]
    width = stacked.shape[1]
    banded = stacked.reshape(spans, width, row_tiles, tile)
    column_ids = jnp.arange(spans * row_tiles, dtype=jnp.int32).reshape(spans, row_tiles)
    picker = (cols[:, None, None] == column_ids[None, :, :]).astype(jnp.bfloat16)
    pieces = jnp.einsum("kbt,bftc->kfc", picker, banded, preferred_element_type=jnp.float32).astype(
        jnp.bfloat16
    )
    products = jnp.einsum("kfc,krc->kfr", pieces, tiles, preferred_element_type=jnp.float32)
    onehot = (rows[None, :] == jnp.arange(row_tiles, dtype=jnp.int32)[:, None]).astype(jnp.float32)
    summed = jnp.einsum("tk,kfr->ftr", onehot, products, precision=lax.Precision.HIGHEST)
    return summed.reshape(width, row_tiles * tile)


def per_device(features_t, weight, bias, cotangent_t, tile_vals, slot_row, slot_col):
    tiles = tile_vals[0, 0]
    rows = slot_row[0, 0]
    cols = slot_col[0, 0]
    tile = tiles.shape[-1]
    row_tiles = features_t.shape[1] // tile
    helper = lax.axis_index("help")
    share = cotangent_t.shape[0]
    partial_value = aggregate(gather_window(features_t), tiles, rows, cols, row_tiles)
    agg_share = lax.psum_scatter(partial_value, "help", scatter_dimension=0, tiled=True).astype(
        jnp.bfloat16
    )
    agg_full = lax.all_gather(agg_share, "help", axis=0, tiled=True)
    weight_cols = lax.dynamic_slice_in_dim(weight, helper * share, share, 1)
    pre = jnp.einsum("io,in->on", weight_cols, agg_full, preferred_element_type=jnp.float32)
    pre = pre + bias[:, None]
    output_t = jax.nn.elu(pre).astype(jnp.bfloat16)
    slope = jnp.where(pre > 0.0, jnp.ones_like(pre), jnp.exp(jnp.minimum(pre, 0.0)))
    grad_pre = (cotangent_t.astype(jnp.float32) * slope).astype(jnp.bfloat16)
    local_weight = jnp.einsum("in,on->io", agg_full, grad_pre, preferred_element_type=jnp.float32)
    local_bias = jnp.sum(grad_pre.astype(jnp.float32), axis=1)
    weight_sum, bias_sum = lax.psum((local_weight, local_bias), "blk")
    nodes_total = features_t.shape[1] * lax.axis_size("blk")
    scale = 1.0 / math.sqrt(nodes_total)
    grad_full = lax.all_gather(grad_pre, "help", axis=0, tiled=True)
    back = jnp.dot(weight, grad_full, preferred_element_type=jnp.float32).astype(jnp.bfloat16)
    back_partial = aggregate(gather_window(back), tiles, rows, cols, row_tiles)
    propagated = lax.psum_scatter(back_partial, "help", scatter_dimension=0, tiled=True)
    return (output_t, propagated, weight_sum * scale, bias_sum * scale)


def solution(mesh):
    placed = (
        P(None, "blk"),
        P(),
        P("help"),
        P("help", "blk"),
        P("blk", "help", None, None, None),
        P("blk", "help", None),
        P("blk", "help", None),
    )
    return jax.shard_map(
        per_device,
        mesh=mesh,
        in_specs=placed,
        out_specs=(P("help", "blk"), P("help", "blk"), P(None, "help"), P("help")),
        check_vma=False,
    )
```

profile of v0, /device:TPU:0, one launch (start us, length us, event | category | flops | bytes accessed | tf_op | source)
XLA Modules:
  0.0 299.2 jit_solution(3390065092874412566)
XLA Ops:
  7.2 0.0 copy-start
  7.2 0.0 reduce-scatter.3.cloned.1.call-start
  7.2 1.6 copy.11
  8.8 3.0 collective-permute-start
  11.8 0.0 collective-permute-start.1
  11.8 4.4 %collective-permute-start.2 = (bf16[256,1536]{0,1:T(8,128)(2,1)S(1)}, bf16[256,1536]{0,1:T(8,128)(2,1)}, u32[]{:S(2)}, u32[]{:S(2)}) collective-permute-start(bf16[256,1536]{0,1:T(8,128)(2,1)S(1)} %copy.11), channel_id=1, source_target_pairs={{2,0},{4,2},{6,4},{8,6},{10,8},{12,10},{14,12},{16,14},{18,16},{20... | collective-permute-start | bytes 2359304 | tf_op jit(solution)/shard_map/ppermute | solution.py:14
  16.2 0.4 collective-permute-start.3
  16.6 0.8 compare_bitcast_fusion
  17.4 0.2 copy.19
  17.6 37.4 %collective-permute-done = bf16[256,1536]{0,1:T(8,128)(2,1)} collective-permute-done((bf16[256,1536]{0,1:T(8,128)(2,1)S(1)}, bf16[256,1536]{0,1:T(8,128)(2,1)}, u32[]{:S(2)}, u32[]{:S(2)}) %collective-permute-start) | collective-permute-done | bytes 786464 | tf_op jit(solution)/shard_map/ppermute | solution.py:14
  55.0 2.1 constant_dynamic-update-slice_fusion.4
  57.1 0.0 collective-permute-done.1
  57.1 2.1 constant_dynamic-update-slice_fusion.3
  59.2 0.9 constant_dynamic-update-slice_fusion.2
  60.1 0.0 collective-permute-done.2
  60.1 2.1 constant_dynamic-update-slice_fusion.1
  62.2 3.9 %collective-permute-done.3 = bf16[256,1536]{0,1:T(8,128)(2,1)} collective-permute-done((bf16[256,1536]{0,1:T(8,128)(2,1)S(1)}, bf16[256,1536]{0,1:T(8,128)(2,1)}, u32[]{:S(2)}, u32[]{:S(2)}) %collective-permute-start.3) | collective-permute-done | bytes 786464 | tf_op jit(solution)/shard_map/ppermute | solution.py:14
  66.2 2.1 constant_dynamic-update-slice_fusion
  68.3 8.2 %copy.20 = bf16[5,256,12,128]{3,2,0,1:T(8,128)(2,1)} copy(bf16[5,256,12,128]{1,3,2,0:T(8,128)(2,1)} %constant_dynamic-update-slice_fusion) | data formatting | bytes 7864320 | tf_op jit(solution)/shard_map/stack | solution.py:24
  76.5 4.0 %fusion.26 = bf16[80,256,128,1]{2,0,3,1:T(8,128)(2,1)S(1)} fusion(pred[80,5,12,1]{0,2,1,3:T(8,128)(4,1)S(1)} %copy.19, bf16[5,256,12,128]{3,2,0,1:T(8,128)(2,1)} %copy.20), kind=kOutput, calls=%fused_computation.42 | convolution fusion | flops 314572800 | bytes 9179840 | tf_op jit(solution)/shard_map/kbt,bftc->kfc/dot_general | solution.py:35
  80.6 0.0 copy-done
  80.6 0.0 copy-start.2
  80.6 1.5 fusion.4
  82.1 0.0 copy-done.2
  82.1 10.9 %fusion.8 = f32[256,12,128]{2,1,0:T(8,128)} fusion(f32[80,256,128]{2,1,0:T(8,128)S(1)} %fusion.4, s32[80]{0:T(128)S(1)} %bitcast.54), kind=kOutput, calls=%fused_computation.12 | convolution fusion | flops 377488320 | bytes 12058944 | tf_op jit(solution)/shard_map/tk,kfr->ftr/dot_general | solution.py:40
  93.1 2.8 copy.16
  95.9 0.0 reduce-scatter.3.cloned.1.call-update
  95.9 0.0 all-reduce.2.cloned.1.call-start
  95.9 29.8 %reduce-scatter.3.cloned.1.call-done = f32[128,1536]{0,1:T(8,128)} async-done(((f32[256,1536]{0,1:T(8,128)}), f32[128,1536]{0,1:T(8,128)}) %reduce-scatter.3.cloned.1.call-update) | async-done | bytes 786448 | tf_op jit(solution)/shard_map/reduce_scatter | solution.py:53
  125.7 1.2 convert_element_type.32
  126.9 11.5 %all_gather.6 = bf16[256,1536]{0,1:T(8,128)(2,1)S(1)} all-gather(bf16[128,1536]{0,1:T(8,128)(2,1)S(1)} %convert_element_type.32), channel_id=1, replica_groups=mesh['blk'=16,'help'=2] {'help'}, dimensions={0}, use_global_device_ids=true | all-gather | bytes 1179648 | tf_op jit(solution)/shard_map/all_gather | solution.py:56
  138.4 0.0 copy-done.1
  138.4 0.0 copy-done.3
  138.4 0.0 copy-done.4
  138.4 2.0 convert_reduce_fusion
  140.4 10.7 %all_gather.7 = bf16[256,1536]{1,0:T(8,128)(2,1)S(1)} all-gather(bf16[128,1536]{1,0:T(8,128)(2,1)S(1)} %get-tuple-element.9), channel_id=1, replica_groups=mesh['blk'=16,'help'=2] {'help'}, dimensions={0}, use_global_device_ids=true | all-gather | bytes 1179648 | tf_op jit(solution)/shard_map/all_gather | solution.py:68
  151.1 0.4 convolution_convert_fusion
  151.6 1.5 collective-permute-start.4
  153.1 0.0 collective-permute-start.5
  153.1 4.4 %collective-permute-start.6 = (bf16[256,1536]{0,1:T(8,128)(2,1)S(1)}, bf16[256,1536]{0,1:T(8,128)(2,1)}, u32[]{:S(2)}, u32[]{:S(2)}) collective-permute-start(bf16[256,1536]{0,1:T(8,128)(2,1)S(1)} %bitcast.51), channel_id=1, source_target_pairs={{2,0},{4,2},{6,4},{8,6},{10,8},{12,10},{14,12},{16,14},{18,16},{20... | collective-permute-start | bytes 2359304 | tf_op jit(solution)/shard_map/ppermute | solution.py:14
  157.5 0.6 collective-permute-start.7
  158.1 1.1 fusion.28
  159.2 0.0 all-reduce.2.cloned.1.call-update
  159.2 0.0 reduce-scatter.5.cloned.1.call-start
  159.2 37.6 %collective-permute-done.4 = bf16[256,1536]{0,1:T(8,128)(2,1)} collective-permute-done((bf16[256,1536]{0,1:T(8,128)(2,1)S(1)}, bf16[256,1536]{0,1:T(8,128)(2,1)}, u32[]{:S(2)}, u32[]{:S(2)}) %collective-permute-start.4) | collective-permute-done | bytes 786464 | tf_op jit(solution)/shard_map/ppermute | solution.py:14
  196.8 2.1 constant_dynamic-update-slice_fusion.9
  198.9 0.0 collective-permute-done.5
  198.9 2.1 constant_dynamic-update-slice_fusion.8
  201.0 0.9 constant_dynamic-update-slice_fusion.7
  202.0 0.0 collective-permute-done.6
  202.0 2.1 constant_dynamic-update-slice_fusion.6
  204.1 2.1 collective-permute-done.7
  206.2 2.1 constant_dynamic-update-slice_fusion.5
  208.3 8.2 %copy.23 = bf16[5,256,12,128]{3,2,0,1:T(8,128)(2,1)} copy(bf16[5,256,12,128]{1,3,2,0:T(8,128)(2,1)} %constant_dynamic-update-slice_fusion.5) | data formatting | bytes 7864320 | tf_op jit(solution)/shard_map/stack | solution.py:24
  216.6 4.0 %fusion.27 = bf16[80,256,128,1]{2,0,3,1:T(8,128)(2,1)S(1)} fusion(pred[80,5,12,1]{0,2,1,3:T(8,128)(4,1)S(1)} %copy.19, bf16[5,256,12,128]{3,2,0,1:T(8,128)(2,1)} %copy.23), kind=kOutput, calls=%fused_computation.43 | convolution fusion | flops 314572800 | bytes 9179840 | tf_op jit(solution)/shard_map/kbt,bftc->kfc/dot_general | solution.py:35
  220.6 1.5 fusion.5
  222.1 10.8 %fusion.11 = f32[256,12,128]{2,1,0:T(8,128)} fusion(f32[80,256,128]{2,1,0:T(8,128)S(1)} %fusion.5, s32[80]{0:T(128)S(1)} %bitcast.55), kind=kOutput, calls=%fused_computation.13 | convolution fusion | flops 377488320 | bytes 12058944 | tf_op jit(solution)/shard_map/tk,kfr->ftr/dot_general | solution.py:40
  232.9 2.7 copy.17
  235.6 0.0 reduce-scatter.5.cloned.1.call-update
  235.7 31.4 %psum.15 = f32[128]{0:T(128)S(1)} all-reduce(f32[128]{0:T(128)S(1)} %copy-done.5), channel_id=1, replica_groups=mesh['blk'=16,'help'=2] {'blk'}, use_global_device_ids=true, to_apply=%region_4.5 | all-reduce | flops 128 | bytes 1024 | tf_op jit(solution)/shard_map/psum | solution.py:65
  267.1 0.5 broadcast_multiply_fusion.1
  267.6 1.6 broadcast_multiply_fusion
  269.2 21.2 %reduce-scatter.5.cloned.1.call-done = f32[128,1536]{0,1:T(8,128)} async-done(((f32[256,1536]{0,1:T(8,128)}), f32[128,1536]{0,1:T(8,128)}) %reduce-scatter.5.cloned.1.call-update) | async-done | bytes 786448 | tf_op jit(solution)/shard_map/reduce_scatter | solution.py:71
  290.4 2.3 copy.18
  (7 shorter events, 0.0 us)
Async XLA Ops:
  7.2 73.4 %copy-start = (bf16[1,1,80,128,128]{4,3,2,1,0:T(8,128)(2,1)S(1)}, bf16[1,1,80,128,128]{4,3,2,1,0:T(8,128)(2,1)}, u32[]{:S(2)}) copy-start(bf16[1,1,80,128,128]{4,3,2,1,0:T(8,128)(2,1)} %param.11) | copy-start | bytes 7864324
  7.2 118.5 %reduce-scatter.3.cloned.1.call-start = ((), (), s32[]{:S(2)}) async-start(), calls=%async_computation.2 | async-start | bytes 2359296 | tf_op jit(solution)/shard_map/reduce_scatter | solution.py:53
  8.8 46.2 %collective-permute-start = (bf16[256,1536]{0,1:T(8,128)(2,1)S(1)}, bf16[256,1536]{0,1:T(8,128)(2,1)}, u32[]{:S(2)}, u32[]{:S(2)}) collective-permute-start(bf16[256,1536]{0,1:T(8,128)(2,1)S(1)} %copy.11), channel_id=1, source_target_pairs={{28,0},{30,2},{0,4},{2,6},{4,8},{6,10},{8,12},{10,14},{12,16},{14,... | collective-permute-start | bytes 2359304 | tf_op jit(solution)/shard_map/ppermute | solution.py:14
  11.8 45.3 %collective-permute-start.1 = (bf16[256,1536]{0,1:T(8,128)(2,1)S(1)}, bf16[256,1536]{0,1:T(8,128)(2,1)}, u32[]{:S(2)}, u32[]{:S(2)}) collective-permute-start(bf16[256,1536]{0,1:T(8,128)(2,1)S(1)} %copy.11), channel_id=1, source_target_pairs={{30,0},{0,2},{2,4},{4,6},{6,8},{8,10},{10,12},{12,14},{14,16},{16,... | collective-permute-start | bytes 2359304 | tf_op jit(solution)/shard_map/ppermute | solution.py:14
  11.8 48.3 %collective-permute-start.2 = (bf16[256,1536]{0,1:T(8,128)(2,1)S(1)}, bf16[256,1536]{0,1:T(8,128)(2,1)}, u32[]{:S(2)}, u32[]{:S(2)}) collective-permute-start(bf16[256,1536]{0,1:T(8,128)(2,1)S(1)} %copy.11), channel_id=1, source_target_pairs={{2,0},{4,2},{6,4},{8,6},{10,8},{12,10},{14,12},{16,14},{18,16},{20... | collective-permute-start | bytes 2359304 | tf_op jit(solution)/shard_map/ppermute | solution.py:14
  16.2 49.9 %collective-permute-start.3 = (bf16[256,1536]{0,1:T(8,128)(2,1)S(1)}, bf16[256,1536]{0,1:T(8,128)(2,1)}, u32[]{:S(2)}, u32[]{:S(2)}) collective-permute-start(bf16[256,1536]{0,1:T(8,128)(2,1)S(1)} %copy.11), channel_id=1, source_target_pairs={{4,0},{6,2},{8,4},{10,6},{12,8},{14,10},{16,12},{18,14},{20,16},{2... | collective-permute-start | bytes 2359304 | tf_op jit(solution)/shard_map/ppermute | solution.py:14
  80.6 1.6 copy-start.2
  93.1 45.4 %copy-start.1 = (bf16[256,256]{1,0:T(8,128)(2,1)S(1)}, bf16[256,256]{1,0:T(8,128)(2,1)}, u32[]{:S(2)}) copy-start(bf16[256,256]{1,0:T(8,128)(2,1)} %param.8) | copy-start | bytes 393220
  93.1 45.4 %copy-start.3 = (bf16[128,1536]{1,0:T(8,128)(2,1)S(1)}, bf16[128,1536]{1,0:T(8,128)(2,1)}, u32[]{:S(2)}) copy-start(bf16[128,1536]{1,0:T(8,128)(2,1)} %param.10) | copy-start | bytes 1179652
  93.1 45.4 %copy-start.4 = (f32[128]{0:T(128)S(1)}, f32[128]{0:T(128)}, u32[]{:S(2)}) copy-start(f32[128]{0:T(128)} %param.9) | copy-start | bytes 1540
  95.9 171.7 %all-reduce.2.cloned.1.call-start = ((), (), s32[]{:S(2)}) async-start(), calls=%async_computation.4 | async-start | bytes 262144 | tf_op jit(solution)/shard_map/psum | solution.py:65
  151.6 45.3 %collective-permute-start.4 = (bf16[256,1536]{0,1:T(8,128)(2,1)S(1)}, bf16[256,1536]{0,1:T(8,128)(2,1)}, u32[]{:S(2)}, u32[]{:S(2)}) collective-permute-start(bf16[256,1536]{0,1:T(8,128)(2,1)S(1)} %bitcast.49), channel_id=1, source_target_pairs={{28,0},{30,2},{0,4},{2,6},{4,8},{6,10},{8,12},{10,14},{12,16},{14,... | collective-permute-start | bytes 2359304 | tf_op jit(solution)/shard_map/ppermute | solution.py:14
  153.1 45.8 %collective-permute-start.5 = (bf16[256,1536]{0,1:T(8,128)(2,1)S(1)}, bf16[256,1536]{0,1:T(8,128)(2,1)}, u32[]{:S(2)}, u32[]{:S(2)}) collective-permute-start(bf16[256,1536]{0,1:T(8,128)(2,1)S(1)} %bitcast.50), channel_id=1, source_target_pairs={{30,0},{0,2},{2,4},{4,6},{6,8},{8,10},{10,12},{12,14},{14,16},{16,... | collective-permute-start | bytes 2359304 | tf_op jit(solution)/shard_map/ppermute | solution.py:14
  153.1 48.9 %collective-permute-start.6 = (bf16[256,1536]{0,1:T(8,128)(2,1)S(1)}, bf16[256,1536]{0,1:T(8,128)(2,1)}, u32[]{:S(2)}, u32[]{:S(2)}) collective-permute-start(bf16[256,1536]{0,1:T(8,128)(2,1)S(1)} %bitcast.51), channel_id=1, source_target_pairs={{2,0},{4,2},{6,4},{8,6},{10,8},{12,10},{14,12},{16,14},{18,16},{20... | collective-permute-start | bytes 2359304 | tf_op jit(solution)/shard_map/ppermute | solution.py:14
  157.5 48.7 %collective-permute-start.7 = (bf16[256,1536]{0,1:T(8,128)(2,1)S(1)}, bf16[256,1536]{0,1:T(8,128)(2,1)}, u32[]{:S(2)}, u32[]{:S(2)}) collective-permute-start(bf16[256,1536]{0,1:T(8,128)(2,1)S(1)} %bitcast.52), channel_id=1, source_target_pairs={{4,0},{6,2},{8,4},{10,6},{12,8},{14,10},{16,12},{18,14},{20,16},{2... | collective-permute-start | bytes 2359304 | tf_op jit(solution)/shard_map/ppermute | solution.py:14
  159.2 131.2 %reduce-scatter.5.cloned.1.call-start = ((), (), s32[]{:S(2)}) async-start(), calls=%async_computation.3 | async-start | bytes 2359296 | tf_op jit(solution)/shard_map/reduce_scatter | solution.py:71
  232.9 2.8 copy-start.5
Sparse Core Ops, SparseCore 0:
  96.0 29.6 reduce-scatter.2
  159.3 100.9 all-reduce.1
  262.6 27.7 reduce-scatter.4
where the time goes:
time: 300 us; the launch traced here: 299 us
  waiting for transfers between devices  132 us (44%)
  blocking collectives  53.7 us (18%)
  local copies, waits for them, and re-layouts  44.7 us (15%)
  matrix products  36.3 us (12%)
  starting transfers between devices  14.5 us (5%)
  between operations  13.8 us (5%)
  other arithmetic  4.07 us (1%)
    ppermute x8, waiting for transfers between devices, shifted(): return lax.ppermute(block, axis, route)  81.1 us
    psum x1, blocking collectives, per_device(): weight_sum, bias_sum = lax.psum((local_weight, local_bias), 'blk')  31.4 us
    reduce_scatter x1, waiting for transfers between devices, per_device(): lax.psum_scatter(partial_value, 'help', scatter_dimension=0, tiled=True)  29.8 us
    dot_general x2, matrix products, aggregate(): jnp.einsum('tk,kfr->ftr', onehot, products, precision=lax.Precision.HIGHEST)  21.7 us
    reduce_scatter x1, waiting for transfers between devices, per_device(): lax.psum_scatter(back_partial, 'help', scatter_dimension=0, tiled=True)  21.2 us
    another operation x4, local copies, waits for them, and re-layouts, gather_window(): stacked = jnp.stack(placed, axis=0)  20.7 us
    unnamed x22, local copies, waits for them, and re-layouts  18.3 us
    ppermute x8, starting transfers between devices, shifted(): return lax.ppermute(block, axis, route)  14.4 us
  transfers between devices with their start and end apart: 11, of which 6 were waited for; matrix products, arithmetic and copies ran while one was open for 16% of the time, Pallas kernels for 0%

commit v1 on v0

v1 whole, which is shorter than its diff:
```python
import functools
import math

import jax
import jax.numpy as jnp
from jax import lax
from jax.experimental import pallas as pl
from jax.experimental.pallas import tpu as pltpu
from jax.sharding import PartitionSpec as P

BAND = 2
SPANS = 2 * BAND + 1
UNROLL = 8
MESH = pl.DeviceIdType.MESH
F32 = jnp.float32
BF16 = jnp.bfloat16


def layer_kernel(
    n_blk, n_help, chunks,
    meta, feat, weight, bias, cot, tiles_hbm,
    out_ref, prop_ref, grads_ref,
    win1, win2, tiles, seg, part, part_in, part2, part2_in, bias_all, cot_all, gp_all, out_all, w_t, wg, wg_in,
    tile_sem, band_send, band_recv, core_send, core_recv, help_send, help_recv, back_send, back_recv, wg_send, wg_recv,
):
    blk = lax.axis_index("blk")
    helper = lax.axis_index("help")
    row_tiles = feat.shape[1] // tiles.shape[-1]
    tile = tiles.shape[-1]
    share = cot.shape[0]
    per = row_tiles // chunks
    steps = n_blk.bit_length() - 1
    core = lax.rem(blk, 2)
    chip = blk // 2
    odd = lax.rem(chip, 2)
    pair = blk + 2 - 4 * odd
    up = lax.rem(blk + 4, n_blk)
    down = lax.rem(blk + n_blk - 4, n_blk)
    relay_to = up + odd * (down - up)
    other = blk + 1 - 2 * core
    own_slot = BAND
    pair_slot = 4 - 4 * odd
    relay_slot = 4 * odd
    ahead_slot = 4 - 4 * core
    own_dst = 1 + 2 * core
    ahead_dst = 3 - 2 * core

    def flip(step):
        bit = 1 << step
        return blk + bit - 2 * bit * lax.rem(blk // bit, 2)

    def helper_at(distance):
        return lax.rem(helper + distance, n_help)

    peers = [up, down, pair] + [flip(s) for s in range(steps) if s != 1]
    barrier = pltpu.get_barrier_semaphore()
    for peer in peers:
        pl.semaphore_signal(barrier, inc=1, device_id={"blk": peer}, device_id_type=MESH)
    for d in range(1, n_help):
        pl.semaphore_signal(barrier, inc=1, device_id={"help": helper_at(d)}, device_id_type=MESH)
    tile_copy = pltpu.make_async_copy(tiles_hbm, tiles, tile_sem)
    tile_copy.start()

    mine = pl.ds(pl.multiple_of(helper * share, share), share)

    def span(slot, j):
        return pl.ds(slot * row_tiles + j * per, per)

    def band_copy(win, stage, kind, j):
        if kind == 0:
            src, dst, to = own_slot, relay_slot, pair
        else:
            src, dst, to = pair_slot, relay_slot, relay_to
        return pltpu.make_async_remote_copy(
            src_ref=win.at[span(src, j)], dst_ref=win.at[span(dst, j)],
            send_sem=band_send.at[stage, kind, j], recv_sem=band_recv.at[stage, kind, j],
            device_id={"blk": to}, device_id_type=MESH,
        )

    def core_copy(win, stage, kind, j):
        if kind == 0:
            src, dst = own_slot, own_dst
        else:
            src, dst = ahead_slot, ahead_dst
        return pltpu.make_async_remote_copy(
            src_ref=win.at[span(src, j)], dst_ref=win.at[span(dst, j)],
            send_sem=core_send.at[stage, kind, j], recv_sem=core_recv.at[stage, kind, j],
            device_id={"blk": other}, device_id_type=MESH,
        )

    def help_copy(src, dst, k, d):
        return pltpu.make_async_remote_copy(
            src_ref=src, dst_ref=dst, send_sem=help_send.at[k, d - 1], recv_sem=help_recv.at[k, d - 1],
            device_id={"help": helper_at(d)}, device_id_type=MESH,
        )

    def cot_copy(d):
        return help_copy(cot_all.at[:, mine, :], cot_all.at[:, mine, :], chunks, d)

    def bias_copy(d):
        return help_copy(bias_all.at[mine, :], bias_all.at[mine, :], chunks + 1, d)

    def part_copy(j, d):
        return help_copy(part.at[pl.ds(j * per, per)], part_in.at[d - 1, pl.ds(j * per, per)], j, d)

    def back_copy(j, d):
        theirs = pl.ds(pl.multiple_of(helper_at(d) * share, share), share)
        return pltpu.make_async_remote_copy(
            src_ref=part2.at[pl.ds(j * per, per), theirs, :], dst_ref=part2_in.at[d - 1, pl.ds(j * per, per)],
            send_sem=back_send.at[j, d - 1], recv_sem=back_recv.at[j, d - 1],
            device_id={"help": helper_at(d)}, device_id_type=MESH,
        )

    def wg_copy(step):
        return pltpu.make_async_remote_copy(
            src_ref=wg.at[step], dst_ref=wg_in.at[step],
            send_sem=wg_send.at[step], recv_sem=wg_recv.at[step],
            device_id={"blk": flip(step)}, device_id_type=MESH,
        )

    def lanes(t):
        return slice(t * tile, (t + 1) * tile)

    pl.semaphore_wait(barrier, len(peers) + n_help - 1)

    for j in range(chunks):
        for t in range(j * per, (j + 1) * per):
            win1[own_slot * row_tiles + t] = feat[:, lanes(t)]
        band_copy(win1, 0, 0, j).start()
    for t in range(row_tiles):
        cot_all[t, mine, :] = cot[:, lanes(t)]
    bias_all[mine, :] = bias[...]
    for d in range(1, n_help):
        cot_copy(d).start()
        bias_copy(d).start()
    for j in range(chunks):
        core_copy(win1, 0, 0, j).start()
    w_t[...] = weight[...].astype(F32).T.astype(BF16)
    wg[0] = jnp.zeros_like(wg.at[0])

    def pass_on(win, stage, j):
        band_copy(win, stage, 0, j).wait_recv()
        band_copy(win, stage, 1, j).start()

    def settle(win, stage):
        for j in range(chunks):
            band_copy(win, stage, 1, j).wait_recv()
            core_copy(win, stage, 1, j).start()
        for j in range(chunks):
            core_copy(win, stage, 0, j).wait_recv()
            core_copy(win, stage, 1, j).wait_recv()

    def aggregate(win, first, last, total):
        def body(group, total):
            for u in range(UNROLL):
                t = group * UNROLL + u
                product = lax.dot_general(
                    win[meta[1, t]], tiles[meta[0, t]], (((1,), (1,)), ((), ())), preferred_element_type=F32
                )
                total = total * meta[2, t].astype(F32) + product
                seg[t] = total
            return total

        return lax.fori_loop(first, last, body, total)

    def row_sum(r):
        return seg[meta[3, r]] * meta[4, r].astype(F32)

    groups = seg.shape[0] // UNROLL
    zero = jnp.zeros(seg.shape[1:], F32)

    for j in range(chunks):
        pass_on(win1, 0, j)
    settle(win1, 0)
    tile_copy.wait()
    aggregate(win1, 0, groups, zero)

    for j in range(chunks):
        for r in range(j * per, (j + 1) * per):
            part[r] = row_sum(r).astype(BF16)
        for d in range(1, n_help):
            part_copy(j, d).start()
    for d in range(1, n_help):
        cot_copy(d).wait_recv()
        bias_copy(d).wait_recv()

    width = weight.shape[0]
    for j in range(chunks):
        for d in range(1, n_help):
            part_copy(j, d).wait_recv()

        def dense(i, carry):
            r = j * per + i
            total = row_sum(r)
            for d in range(1, n_help):
                total = total + part_in[d - 1, r].astype(F32)
            agg = total.astype(BF16)
            pre = jnp.dot(w_t[...], agg, preferred_element_type=F32) + bias_all[...]
            ex = jnp.exp(jnp.minimum(pre, 0.0))
            out_all[r] = jnp.where(pre > 0.0, pre, ex - 1.0).astype(BF16)
            grad = (cot_all[r].astype(F32) * ex).astype(BF16)
            gp_all[r] = grad
            back = jnp.dot(weight[...], grad, preferred_element_type=F32).astype(BF16)
            win2[own_slot * row_tiles + r] = back
            held = gp_all[r, mine, :]
            wg[0, :, pl.ds(0, width)] += lax.dot_general(
                held, agg, (((1,), (1,)), ((), ())), preferred_element_type=F32
            )
            wg[0, :, pl.ds(width, tile)] += held.astype(F32)
            return carry

        lax.fori_loop(0, per, dense, 0)
        band_copy(win2, 1, 0, j).start()
        core_copy(win2, 1, 0, j).start()
        if j > 0:
            pass_on(win2, 1, j - 1)
    wg_copy(0).start()
    for t in range(row_tiles):
        out_ref[:, lanes(t)] = out_all[t, mine, :]
    pass_on(win2, 1, chunks - 1)

    def wg_turn(step):
        wg_copy(step).wait_recv()
        wg[step + 1] = wg[step] + wg_in[step]
        if step + 1 < steps:
            wg_copy(step + 1).start()

    settle(win2, 1)
    wg_turn(0)
    half = groups // 2
    total = aggregate(win2, 0, half, zero)
    wg_turn(1)
    aggregate(win2, half, groups, total)

    for j in range(chunks):
        for r in range(j * per, (j + 1) * per):
            part2[r] = row_sum(r).astype(BF16)
            prop_ref[:, lanes(r)] = seg[meta[3, r], mine, :] * meta[4, r].astype(F32)
        for d in range(1, n_help):
            back_copy(j, d).start()
    wg_turn(2)
    for j in range(chunks):
        for d in range(1, n_help):
            back_copy(j, d).wait_recv()
        for r in range(j * per, (j + 1) * per):
            for d in range(1, n_help):
                prop_ref[:, lanes(r)] += part2_in[d - 1, r].astype(F32)
    for s in range(3, steps):
        wg_turn(s)
    grads_ref[...] = wg[steps]

    for stage, win in ((0, win1), (1, win2)):
        for j in range(chunks):
            for kind in range(2):
                band_copy(win, stage, kind, j).wait_send()
                core_copy(win, stage, kind, j).wait_send()
    for d in range(1, n_help):
        cot_copy(d).wait_send()
        bias_copy(d).wait_send()
        for j in range(chunks):
            part_copy(j, d).wait_send()
            back_copy(j, d).wait_send()
    for s in range(steps):
        wg_copy(s).wait_send()


def slot_table(rows, cols, row_tiles):
    slots = rows.shape[0]
    index = jnp.arange(slots, dtype=jnp.int32)
    key = rows * slots + index
    rank = jnp.sum((key[None, :] < key[:, None]).astype(jnp.int32), axis=1)
    placed = (rank[None, :] == index[:, None]).astype(jnp.int32)
    order = jnp.sum(placed * index[None, :], axis=1)
    col = jnp.sum(placed * cols[None, :], axis=1)
    head = jnp.sum(((rows[None, :] == rows[:, None]) & (index[None, :] < index[:, None])).astype(jnp.int32), axis=1)
    keep = jnp.sum(placed * (head > 0).astype(jnp.int32)[None, :], axis=1)
    tiles = jnp.arange(slots, dtype=jnp.int32)[:, None]
    last = jnp.maximum(jnp.sum((rows[None, :] <= tiles).astype(jnp.int32), axis=1) - 1, 0)
    has = jnp.max((rows[None, :] == tiles).astype(jnp.int32), axis=1)
    table = jnp.stack([order, col, keep, last, has])
    return jnp.pad(table, ((0, 3), (0, 128 - slots)))


def per_device(n_blk, n_help, features_t, weight, bias, cotangent_t, tile_vals, slot_row, slot_col):
    tiles = tile_vals[0, 0]
    slots, tile = tiles.shape[0], tiles.shape[-1]
    width, nodes = features_t.shape
    row_tiles = nodes // tile
    share = cotangent_t.shape[0]
    chunks = 4 if row_tiles % 4 == 0 else 1
    steps = n_blk.bit_length() - 1
    peers = n_help - 1
    table = slot_table(slot_row[0, 0], slot_col[0, 0], row_tiles)
    bias_wide = jnp.broadcast_to(bias[:, None], (share, tile))
    vmem = pl.BlockSpec(memory_space=pltpu.VMEM)
    dma = pltpu.SemaphoreType.DMA
    output_t, propagated, grads = pl.pallas_call(
        functools.partial(layer_kernel, n_blk, n_help, chunks),
        out_shape=(
            jax.ShapeDtypeStruct((share, nodes), BF16),
            jax.ShapeDtypeStruct((share, nodes), F32),
            jax.ShapeDtypeStruct((share, width + tile), F32),
        ),
        in_specs=[pl.BlockSpec(memory_space=pltpu.SMEM), vmem, vmem, vmem, vmem, pl.BlockSpec(memory_space=pl.ANY)],
        out_specs=(vmem, vmem, vmem),
        scratch_shapes=[
            pltpu.VMEM((SPANS * row_tiles, width, tile), BF16),
            pltpu.VMEM((SPANS * row_tiles, width, tile), BF16),
            pltpu.VMEM((slots, tile, tile), BF16),
            pltpu.VMEM((slots, width, tile), F32),
            pltpu.VMEM((row_tiles, width, tile), BF16),
            pltpu.VMEM((peers, row_tiles, width, tile), BF16),
            pltpu.VMEM((row_tiles, width, tile), BF16),
            pltpu.VMEM((peers, row_tiles, share, tile), BF16),
            pltpu.VMEM((width, tile), F32),
            pltpu.VMEM((row_tiles, width, tile), BF16),
            pltpu.VMEM((row_tiles, width, tile), BF16),
            pltpu.VMEM((row_tiles, width, tile), BF16),
            pltpu.VMEM((width, width), BF16),
            pltpu.VMEM((steps + 1, share, width + tile), F32),
            pltpu.VMEM((steps, share, width + tile), F32),
            dma,
            dma((2, 2, chunks)),
            dma((2, 2, chunks)),
            dma((2, 2, chunks)),
            dma((2, 2, chunks)),
            dma((chunks + 2, peers)),
            dma((chunks + 2, peers)),
            dma((chunks, peers)),
            dma((chunks, peers)),
            dma((steps,)),
            dma((steps,)),
        ],
        compiler_params=pltpu.CompilerParams(
            collective_id=0, has_side_effects=True, vmem_limit_bytes=48 * 1024 * 1024
        ),
    )(table, features_t, weight, bias_wide, cotangent_t, tiles)
    scale = 1.0 / math.sqrt(nodes * n_blk)
    weight_grad = grads[:, :width].T * scale
    bias_grad = jnp.sum(grads[:, width:], axis=1) * scale
    return (output_t, propagated, weight_grad, bias_grad)


def solution(mesh):
    placed = (
        P(None, "blk"),
        P(),
        P("help"),
        P("help", "blk"),
        P("blk", "help", None, None, None),
        P("blk", "help", None),
        P("blk", "help", None),
    )
    return jax.shard_map(
        functools.partial(per_device, mesh.shape["blk"], mesh.shape["help"]),
        mesh=mesh,
        in_specs=placed,
        out_specs=(P("help", "blk"), P("help", "blk"), P(None, "help"), P("help")),
        check_vma=False,
    )
```

time: 300 us -> 104 us (0.35)
  waiting for transfers between devices: 132 us -> 0 us
  Pallas kernels: 0 us -> 91.5 us
  blocking collectives: 53.7 us -> 0 us
  local copies, waits for them, and re-layouts: 44.7 us -> 7.92 us
  matrix products: 36.3 us -> 0 us
  starting transfers between devices: 14.5 us -> 0 us
  between operations: 13.8 us -> 0.69 us
    pallas_call x0 -> x1, Pallas kernels: none -> 91.5 us  [per_device(): pl.pallas_call(functools.partial(layer_kernel, n_blk, n_help, chunks), ou...]
    ppermute x8 -> x0, waiting for transfers between devices: 81.1 us -> none  [shifted(): return lax.ppermute(block, axis, route)]
    reduce_scatter x2 -> x0, waiting for transfers between devices: 51 us -> none  [the longest x1 29.8 us: per_device(): lax.psum_scatter(partial_value, 'help', scatter_dimension=0, tiled=True)]
    dot_general x9 -> x0, matrix products: 36.3 us -> none  [the longest x2 21.7 us: aggregate(): jnp.einsum('tk,kfr->ftr', onehot, products, precision=lax.Precision.HIGHEST)]
    psum x1 -> x0, blocking collectives: 31.4 us -> none  [per_device(): weight_sum, bias_sum = lax.psum((local_weight, local_bias), 'blk')]
    all_gather x2 -> x0, blocking collectives: 22.3 us -> none  [the longest x1 11.5 us: per_device(): agg_full = lax.all_gather(agg_share, 'help', axis=0, tiled=True)]
    another operation x4 -> x1, local copies, waits for them, and re-layouts: 20.7 us -> 0.03 us  [slot_table(): table = jnp.stack([order, col, keep, last, has])]
    ppermute x8 -> x0, starting transfers between devices: 14.4 us -> none  [shifted(): return lax.ppermute(block, axis, route)]
  transfers between devices with their start and end apart: 11 -> 0, of which waited for: 6 -> 0; matrix products, arithmetic and copies ran while one was open for 16% -> 0% of each run, Pallas kernels for 0% -> 0%
where the time goes in v1:
time: 104 us; the launch traced here: 103 us
  Pallas kernels  91.5 us (88%)
  local copies, waits for them, and re-layouts  7.92 us (8%)
  other arithmetic  3.24 us (3%)
    pallas_call x1, Pallas kernels, per_device(): pl.pallas_call(functools.partial(layer_kernel, n_blk, n_help, chunks), ou...  91.5 us
    unnamed x11, local copies, waits for them, and re-layouts  7.15 us

profile of v1, /device:TPU:0, one launch (start us, length us, event | category | flops | bytes accessed | tf_op | source)
XLA Modules:
  0.0 103.4 jit_solution(1604841640129693359)
XLA Ops:
  0.6 0.7 iota_add_fusion
  1.3 0.2 convert_reduce_fusion.3
  1.5 1.0 convert_reduce_fusion
  2.4 0.8 select_reduce_fusion
  3.3 0.7 broadcast_in_dim.2.bias
  4.0 0.0 copy-start
  4.0 1.7 %copy-done = bf16[1,1,80,128,128]{4,3,2,1,0:T(8,128)(2,1)S(1)} copy-done((bf16[1,1,80,128,128]{4,3,2,1,0:T(8,128)(2,1)S(1)}, bf16[1,1,80,128,128]{4,3,2,1,0:T(8,128)(2,1)}, u32[]{:S(2)}) %copy-start) | copy-done | bytes 2621464
  5.8 0.0 copy-start.1
  5.8 1.1 %copy-done.1 = bf16[256,1536]{1,0:T(8,128)(2,1)S(1)} copy-done((bf16[256,1536]{1,0:T(8,128)(2,1)S(1)}, bf16[256,1536]{1,0:T(8,128)(2,1)}, u32[]{:S(2)}) %copy-start.1) | copy-done | bytes 786456
  6.9 0.0 copy-start.2
  6.9 1.0 copy-done.2
  7.9 0.0 copy-start.3
  7.9 0.9 copy-done.3
  8.8 91.5 %shard_map.102 = (bf16[128,1536]{1,0:T(8,128)(2,1)S(1)}, f32[128,1536]{1,0:T(8,128)S(1)}, f32[128,384]{1,0:T(8,128)S(1)}) custom-call(s32[8,128]{1,0:T(8,128)S(1)} %pad.4.meta, bf16[256,1536]{1,0:T(8,128)(2,1)S(1)} %copy-done.1, bf16[256,256]{1,0:T(8,128)(2,1)S(1)} %copy-done.3, f32[128,128]{1,0:T(8,128)S(1)} %broadcast_in_dim.2.bias, ...), custom_call_target="tpu_custom_call" | custom-call | tf_op jit(solution)/shard_map/pallas_call | solution.py:297
  100.3 0.1 slice_reduce_fusion
  100.5 0.8 copy.12
  101.2 0.5 broadcast_multiply_fusion
  101.7 0.7 copy.15
  102.5 0.9 copy.16
  (5 shorter events, 0.1 us)
Async XLA Ops:
  4.0 1.8 %copy-start = (bf16[1,1,80,128,128]{4,3,2,1,0:T(8,128)(2,1)S(1)}, bf16[1,1,80,128,128]{4,3,2,1,0:T(8,128)(2,1)}, u32[]{:S(2)}) copy-start(bf16[1,1,80,128,128]{4,3,2,1,0:T(8,128)(2,1)} %param.11) | copy-start | bytes 7864324
  5.8 1.1 %copy-start.1 = (bf16[256,1536]{1,0:T(8,128)(2,1)S(1)}, bf16[256,1536]{1,0:T(8,128)(2,1)}, u32[]{:S(2)}) copy-start(bf16[256,1536]{1,0:T(8,128)(2,1)} %feat.1) | copy-start | bytes 2359300
  6.9 1.0 copy-start.2
  7.9 0.9 copy-start.3

commit v2 on v1

--- a/solution.py
+++ b/solution.py
@@ -18,16 +18,17 @@
 
 def layer_kernel(
     n_blk, n_help, chunks,
-    meta, feat, weight, bias, cot, tiles_hbm,
+    meta, feat_hbm, weight_hbm, bias_hbm, cot_hbm, tiles_hbm,
     out_ref, prop_ref, grads_ref,
+    feat, weight, bias_wide, cot,
     win1, win2, tiles, seg, part, part_in, part2, part2_in, bias_all, cot_all, gp_all, out_all, w_t, wg, wg_in,
-    tile_sem, band_send, band_recv, core_send, core_recv, help_send, help_recv, back_send, back_recv, wg_send, wg_recv,
+    sums, feat_sem, tile_sem, weight_sem, cot_sem, bias_sem, band_send, band_recv, core_send, core_recv, help_send, help_recv, back_send, back_recv, wg_send, wg_recv,
 ):
     blk = lax.axis_index("blk")
     helper = lax.axis_index("help")
     row_tiles = feat.shape[1] // tiles.shape[-1]
     tile = tiles.shape[-1]
-    share = cot.shape[0]
+    share = out_ref.shape[0]
     per = row_tiles // chunks
     steps = n_blk.bit_length() - 1
     core = lax.rem(blk, 2)
@@ -52,6 +53,20 @@
     def helper_at(distance):
         return lax.rem(helper + distance, n_help)
 
+    mine = pl.ds(pl.multiple_of(helper * share, share), share)
+
+    def feat_copy(j):
+        part_of = (slice(None), slice(j * per * tile, (j + 1) * per * tile))
+        return pltpu.make_async_copy(feat_hbm.at[part_of], feat.at[part_of], feat_sem.at[j])
+
+    def cot_load(t):
+        return pltpu.make_async_copy(cot_hbm.at[:, lanes(t)], cot_all.at[t, mine, :], cot_sem.at[t])
+
+    def lanes(t):
+        return slice(t * tile, (t + 1) * tile)
+
+    for j in range(chunks):
+        feat_copy(j).start()
     peers = [up, down, pair] + [flip(s) for s in range(steps) if s != 1]
     barrier = pltpu.get_barrier_semaphore()
     for peer in peers:
@@ -59,9 +74,8 @@
     for d in range(1, n_help):
         pl.semaphore_signal(barrier, inc=1, device_id={"help": helper_at(d)}, device_id_type=MESH)
     tile_copy = pltpu.make_async_copy(tiles_hbm, tiles, tile_sem)
-    tile_copy.start()
-
-    mine = pl.ds(pl.multiple_of(helper * share, share), share)
+    weight_copy = pltpu.make_async_copy(weight_hbm, weight, weight_sem)
+    bias_load = pltpu.make_async_copy(bias_hbm, bias_all.at[mine, :], bias_sem)
 
     def span(slot, j):
         return pl.ds(slot * row_tiles + j * per, per)
@@ -118,24 +132,28 @@
             device_id={"blk": flip(step)}, device_id_type=MESH,
         )
 
-    def lanes(t):
-        return slice(t * tile, (t + 1) * tile)
-
-    pl.semaphore_wait(barrier, len(peers) + n_help - 1)
-
-    for j in range(chunks):
+    weight_copy.start()
+    bias_load.start()
+    for t in range(row_tiles):
+        cot_load(t).start()
+    tile_copy.start()
+    for j in range(chunks):
+        feat_copy(j).wait()
         for t in range(j * per, (j + 1) * per):
-            win1[own_slot * row_tiles + t] = feat[:, lanes(t)]
+            win1[own_slot * row_tiles + t] = feat[:, lanes(t)].T
+        if j == 0:
+            pl.semaphore_wait(barrier, len(peers) + n_help - 1)
         band_copy(win1, 0, 0, j).start()
     for t in range(row_tiles):
-        cot_all[t, mine, :] = cot[:, lanes(t)]
-    bias_all[mine, :] = bias[...]
+        cot_load(t).wait()
+    bias_load.wait()
     for d in range(1, n_help):
         cot_copy(d).start()
         bias_copy(d).start()
     for j in range(chunks):
         core_copy(win1, 0, 0, j).start()
-    w_t[...] = weight[...].astype(F32).T.astype(BF16)
+    weight_copy.wait()
+    w_t[...] = weight[...].T
     wg[0] = jnp.zeros_like(wg.at[0])
 
     def pass_on(win, stage, j):
@@ -154,9 +172,7 @@
         def body(group, total):
             for u in range(UNROLL):
                 t = group * UNROLL + u
-                product = lax.dot_general(
-                    win[meta[1, t]], tiles[meta[0, t]], (((1,), (1,)), ((), ())), preferred_element_type=F32
-                )
+                product = jnp.dot(tiles[meta[0, t]], win[meta[1, t]], preferred_element_type=F32)
                 total = total * meta[2, t].astype(F32) + product
                 seg[t] = total
             return total
@@ -185,31 +201,26 @@
         bias_copy(d).wait_recv()
 
     width = weight.shape[0]
+    for t in range(row_tiles):
+        cot[t] = cot_all[t].T
+    bias_wide[...] = bias_all[...].T
     for j in range(chunks):
         for d in range(1, n_help):
             part_copy(j, d).wait_recv()
-
-        def dense(i, carry):
-            r = j * per + i
+        for r in range(j * per, (j + 1) * per):
             total = row_sum(r)
             for d in range(1, n_help):
                 total = total + part_in[d - 1, r].astype(F32)
             agg = total.astype(BF16)
-            pre = jnp.dot(w_t[...], agg, preferred_element_type=F32) + bias_all[...]
+            pre = jnp.dot(agg, weight[...], preferred_element_type=F32) + bias_wide[...]
             ex = jnp.exp(jnp.minimum(pre, 0.0))
-            out_all[r] = jnp.where(pre > 0.0, pre, ex - 1.0).astype(BF16)
-            grad = (cot_all[r].astype(F32) * ex).astype(BF16)
-            gp_all[r] = grad
-            back = jnp.dot(weight[...], grad, preferred_element_type=F32).astype(BF16)
-            win2[own_slot * row_tiles + r] = back
+            grad = (cot[r].astype(F32) * ex).astype(BF16)
+            win2[own_slot * row_tiles + r] = jnp.dot(grad, w_t[...], preferred_element_type=F32).astype(BF16)
+            out_all[r] = jnp.where(pre > 0.0, pre, ex - 1.0).astype(BF16).T
+            gp_all[r] = grad.T
             held = gp_all[r, mine, :]
-            wg[0, :, pl.ds(0, width)] += lax.dot_general(
-                held, agg, (((1,), (1,)), ((), ())), preferred_element_type=F32
-            )
+            wg[0, :, pl.ds(0, width)] += jnp.dot(held, agg, preferred_element_type=F32)
             wg[0, :, pl.ds(width, tile)] += held.astype(F32)
-            return carry
-
-        lax.fori_loop(0, per, dense, 0)
         band_copy(win2, 1, 0, j).start()
         core_copy(win2, 1, 0, j).start()
         if j > 0:
@@ -234,8 +245,10 @@
 
     for j in range(chunks):
         for r in range(j * per, (j + 1) * per):
-            part2[r] = row_sum(r).astype(BF16)
-            prop_ref[:, lanes(r)] = seg[meta[3, r], mine, :] * meta[4, r].astype(F32)
+            turned = row_sum(r).T
+            part2[r] = turned.astype(BF16)
+            sums[r] = turned
+            prop_ref[:, lanes(r)] = sums[r, mine, :]
         for d in range(1, n_help):
             back_copy(j, d).start()
     wg_turn(2)
@@ -287,7 +300,7 @@
     width, nodes = features_t.shape
     row_tiles = nodes // tile
     share = cotangent_t.shape[0]
-    chunks = 4 if row_tiles % 4 == 0 else 1
+    chunks = row_tiles // 2 if row_tiles % 2 == 0 else row_tiles
     steps = n_blk.bit_length() - 1
     peers = n_help - 1
     table = slot_table(slot_row[0, 0], slot_col[0, 0], row_tiles)
@@ -301,15 +314,19 @@
             jax.ShapeDtypeStruct((share, nodes), F32),
             jax.ShapeDtypeStruct((share, width + tile), F32),
         ),
-        in_specs=[pl.BlockSpec(memory_space=pltpu.SMEM), vmem, vmem, vmem, vmem, pl.BlockSpec(memory_space=pl.ANY)],
+        in_specs=[pl.BlockSpec(memory_space=pltpu.SMEM)] + [pl.BlockSpec(memory_space=pl.ANY)] * 5,
         out_specs=(vmem, vmem, vmem),
         scratch_shapes=[
-            pltpu.VMEM((SPANS * row_tiles, width, tile), BF16),
-            pltpu.VMEM((SPANS * row_tiles, width, tile), BF16),
+            pltpu.VMEM((width, nodes), BF16),
+            pltpu.VMEM((width, width), BF16),
+            pltpu.VMEM((tile, width), F32),
+            pltpu.VMEM((row_tiles, tile, width), BF16),
+            pltpu.VMEM((SPANS * row_tiles, tile, width), BF16),
+            pltpu.VMEM((SPANS * row_tiles, tile, width), BF16),
             pltpu.VMEM((slots, tile, tile), BF16),
-            pltpu.VMEM((slots, width, tile), F32),
-            pltpu.VMEM((row_tiles, width, tile), BF16),
-            pltpu.VMEM((peers, row_tiles, width, tile), BF16),
+            pltpu.VMEM((slots, tile, width), F32),
+            pltpu.VMEM((row_tiles, tile, width), BF16),
+            pltpu.VMEM((peers, row_tiles, tile, width), BF16),
             pltpu.VMEM((row_tiles, width, tile), BF16),
             pltpu.VMEM((peers, row_tiles, share, tile), BF16),
             pltpu.VMEM((width, tile), F32),
@@ -319,6 +336,11 @@
             pltpu.VMEM((width, width), BF16),
             pltpu.VMEM((steps + 1, share, width + tile), F32),
             pltpu.VMEM((steps, share, width + tile), F32),
+            pltpu.VMEM((row_tiles, width, tile), F32),
+            dma((chunks,)),
+            dma,
+            dma,
+            dma((row_tiles,)),
             dma,
             dma((2, 2, chunks)),
             dma((2, 2, chunks)),
@@ -332,7 +354,7 @@
             dma((steps,)),
         ],
         compiler_params=pltpu.CompilerParams(
-            collective_id=0, has_side_effects=True, vmem_limit_bytes=48 * 1024 * 1024
+            collective_id=0, has_side_effects=True, vmem_limit_bytes=60 * 1024 * 1024
         ),
     )(table, features_t, weight, bias_wide, cotangent_t, tiles)
     scale = 1.0 / math.sqrt(nodes * n_blk)

time: 104 us -> 102 us (0.981)
  Pallas kernels: 91.5 us -> 89 us
  other arithmetic: 3.24 us -> 4.99 us
  local copies, waits for them, and re-layouts: 7.92 us -> 6.59 us
    unnamed x11 -> x3, local copies, waits for them, and re-layouts: 7.15 us -> 4.59 us
    pallas_call x1, Pallas kernels: 91.5 us -> 89 us  [per_device(): pl.pallas_call(functools.partial(layer_kernel, n_blk, n_help, chunks), ou...]
where the time goes in v2:
time: 102 us; the launch traced here: 101 us
  Pallas kernels  89 us (87%)
  local copies, waits for them, and re-layouts  6.59 us (6%)
  other arithmetic  4.99 us (5%)
    pallas_call x1, Pallas kernels, per_device(): pl.pallas_call(functools.partial(layer_kernel, n_blk, n_help, chunks), ou...  89 us
    unnamed x3, local copies, waits for them, and re-layouts  4.59 us

profile of v2, /device:TPU:0, one launch (start us, length us, event | category | flops | bytes accessed | tf_op | source)
XLA Modules:
  0.0 101.3 jit_solution(18264174623303718496)
XLA Ops:
  0.6 0.7 iota_add_fusion
  1.3 0.2 convert_reduce_fusion.3
  1.5 1.0 convert_reduce_fusion
  2.4 0.8 select_reduce_fusion
  3.3 0.6 pad.4.meta
  3.9 1.4 %broadcast_in_dim.2.bias_hbm = f32[128,128]{1,0:T(8,128)} broadcast(f32[128]{0:T(128)} %param.9), dimensions={0} | broadcast | bytes 66048 | tf_op jit(solution)/shard_map/broadcast_in_dim | solution.py:307
  5.3 89.0 %shard_map.102 = (bf16[128,1536]{1,0:T(8,128)(2,1)}, f32[128,1536]{1,0:T(8,128)}, f32[128,384]{1,0:T(8,128)}) custom-call(s32[8,128]{1,0:T(8,128)} %pad.4.meta, bf16[256,1536]{1,0:T(8,128)(2,1)} %feat_hbm.1, bf16[256,256]{1,0:T(8,128)(2,1)} %weight_hbm.1, f32[128,128]{1,0:T(8,128)} %broadcast_in_dim.2.bias_hbm, bf16[128,1536]{1,0:T(8,128)(2,1)} %cot_hbm.1, ...), custom_call_target="tpu_custom_call" | custom-call | tf_op jit(solution)/shard_map/pallas_call | solution.py:310
  94.3 0.9 slice_reduce_fusion
  95.3 0.9 multiply_bitcast_fusion
  96.2 0.8 copy.12
  97.0 0.5 broadcast_multiply_fusion
  97.5 1.8 %copy.15 = bf16[128,1536]{1,0:T(8,128)(2,1)} copy(bf16[128,1536]{1,0:T(8,128)(2,1)} %get-tuple-element.28) | data formatting | bytes 786432
  99.2 2.1 %copy.16 = f32[128,1536]{1,0:T(8,128)} copy(f32[128,1536]{1,0:T(8,128)} %get-tuple-element.29) | data formatting | bytes 1572864
  (3 shorter events, 0.0 us)

commit v3 on v2

v3 whole, which is shorter than its diff:
```python
import functools
import math

import jax
import jax.numpy as jnp
from jax import lax
from jax.experimental import pallas as pl
from jax.experimental.pallas import tpu as pltpu
from jax.sharding import PartitionSpec as P

BAND = 2
SPANS = 2 * BAND + 1
UNROLL = 8
HALVES = 2
VMEM_MIB = 60
MESH = pl.DeviceIdType.MESH
F32 = jnp.float32
BF16 = jnp.bfloat16


def layer_kernel(
    n_blk, n_help, chunks,
    rows_hbm, cols_hbm, feat_hbm, weight_hbm, bias_hbm, cot_hbm, tiles_hbm,
    out_ref, prop_ref, grads_ref,
    rows, cols, bias, table, meta, feat, weight, bias_wide, cot,
    win1a, win1b, win2a, win2b, tiles, seg, part, part_in, part2, part2_in, bias_all, cot_all, gp_all, out_all, w_t, wg, wg_in,
    sums, small_sem, feat_sem, tile_sem, weight_sem, cot_sem,
    band_send, band_recv, core_send, core_recv, help_send, help_recv, side_send, side_recv,
    back_send, back_recv, wg_send, wg_recv,
):
    blk = lax.axis_index("blk")
    helper = lax.axis_index("help")
    row_tiles = feat.shape[1] // tiles.shape[-1]
    slots = tiles.shape[0]
    tile = tiles.shape[-1]
    width = weight.shape[0]
    half = width // HALVES
    share = out_ref.shape[0]
    per = row_tiles // chunks
    steps = n_blk.bit_length() - 1
    core = lax.rem(blk, 2)
    chip = blk // 2
    odd = lax.rem(chip, 2)
    pair = blk + 2 - 4 * odd
    up = lax.rem(blk + 4, n_blk)
    down = lax.rem(blk + n_blk - 4, n_blk)
    relay_to = up + odd * (down - up)
    other = blk + 1 - 2 * core
    own_slot = BAND
    pair_slot = 4 - 4 * odd
    relay_slot = 4 * odd
    ahead_slot = 4 - 4 * core
    own_dst = 1 + 2 * core
    ahead_dst = 3 - 2 * core
    own_half = (helper * share) // half
    turn_half = (1 - own_half, own_half)
    win1, win2 = (win1a, win1b), (win2a, win2b)

    def flip(step):
        bit = 1 << step
        return blk + bit - 2 * bit * lax.rem(blk // bit, 2)

    def helper_at(distance):
        return lax.rem(helper + distance, n_help)

    def lanes(t):
        return slice(t * tile, (t + 1) * tile)

    mine = pl.ds(pl.multiple_of(helper * share, share), share)

    def feat_copy(h, j):
        piece = (slice(h * half, (h + 1) * half), slice(j * per * tile, (j + 1) * per * tile))
        return pltpu.make_async_copy(feat_hbm.at[piece], feat.at[piece], feat_sem.at[h, j])

    def cot_load(t):
        return pltpu.make_async_copy(cot_hbm.at[:, lanes(t)], cot_all.at[t, mine, :], cot_sem.at[t])

    for h in range(HALVES):
        for j in range(chunks):
            feat_copy(h, j).start()
    peers = [up, down, pair] + [flip(s) for s in range(steps) if s != 1]
    barrier = pltpu.get_barrier_semaphore()
    for peer in peers:
        pl.semaphore_signal(barrier, inc=1, device_id={"blk": peer}, device_id_type=MESH)
    for d in range(1, n_help):
        pl.semaphore_signal(barrier, inc=1, device_id={"help": helper_at(d)}, device_id_type=MESH)
    small = [
        pltpu.make_async_copy(rows_hbm, rows, small_sem.at[0]),
        pltpu.make_async_copy(cols_hbm, cols, small_sem.at[1]),
        pltpu.make_async_copy(bias_hbm, bias, small_sem.at[2]),
    ]
    table_copy = pltpu.make_async_copy(table, meta, small_sem.at[3])
    tile_copy = pltpu.make_async_copy(tiles_hbm, tiles, tile_sem)
    weight_copy = pltpu.make_async_copy(weight_hbm, weight, weight_sem)

    def span(slot, j):
        return pl.ds(slot * row_tiles + j * per, per)

    def band_copy(win, stage, kind, turn, j):
        if kind == 0:
            src, dst, to = own_slot, relay_slot, pair
        else:
            src, dst, to = pair_slot, relay_slot, relay_to
        return pltpu.make_async_remote_copy(
            src_ref=win[turn].at[span(src, j)], dst_ref=win[turn].at[span(dst, j)],
            send_sem=band_send.at[stage, kind, turn, j], recv_sem=band_recv.at[stage, kind, turn, j],
            device_id={"blk": to}, device_id_type=MESH,
        )

    def core_copy(win, stage, kind, turn, j):
        if kind == 0:
            src, dst = own_slot, own_dst
        else:
            src, dst = ahead_slot, ahead_dst
        return pltpu.make_async_remote_copy(
            src_ref=win[turn].at[span(src, j)], dst_ref=win[turn].at[span(dst, j)],
            send_sem=core_send.at[stage, kind, turn, j], recv_sem=core_recv.at[stage, kind, turn, j],
            device_id={"blk": other}, device_id_type=MESH,
        )

    def side_copy(ref, k, d):
        return pltpu.make_async_remote_copy(
            src_ref=ref, dst_ref=ref, send_sem=side_send.at[k, d - 1], recv_sem=side_recv.at[k, d - 1],
            device_id={"help": helper_at(d)}, device_id_type=MESH,
        )

    def cot_copy(d):
        return side_copy(cot_all.at[:, mine, :], 0, d)

    def bias_copy(d):
        return side_copy(bias_all.at[mine, :], 1, d)

    def part_copy(h, j, d):
        piece = pl.ds(j * per, per)
        return pltpu.make_async_remote_copy(
            src_ref=part.at[h, piece], dst_ref=part_in.at[d - 1, h, piece],
            send_sem=help_send.at[h, j, d - 1], recv_sem=help_recv.at[h, j, d - 1],
            device_id={"help": helper_at(d)}, device_id_type=MESH,
        )

    def back_copy(j, d):
        theirs = pl.ds(pl.multiple_of(helper_at(d) * share, share), share)
        piece = pl.ds(j * per, per)
        return pltpu.make_async_remote_copy(
            src_ref=part2.at[piece, theirs, :], dst_ref=part2_in.at[d - 1, piece],
            send_sem=back_send.at[j, d - 1], recv_sem=back_recv.at[j, d - 1],
            device_id={"help": helper_at(d)}, device_id_type=MESH,
        )

    def wg_copy(step):
        return pltpu.make_async_remote_copy(
            src_ref=wg.at[step], dst_ref=wg_in.at[step],
            send_sem=wg_send.at[step], recv_sem=wg_recv.at[step],
            device_id={"blk": flip(step)}, device_id_type=MESH,
        )

    for copy in small:
        copy.start()
    weight_copy.start()
    for t in range(row_tiles):
        cot_load(t).start()
    tile_copy.start()
    for h in range(HALVES):
        for j in range(chunks):
            feat_copy(h, j).wait()
            for t in range(j * per, (j + 1) * per):
                win1[h][own_slot * row_tiles + t] = feat[h * half : (h + 1) * half, lanes(t)].T
            if h == 0 and j == 0:
                pl.semaphore_wait(barrier, len(peers) + n_help - 1)
            band_copy(win1, 0, 0, h, j).start()
        for j in range(chunks):
            core_copy(win1, 0, 0, h, j).start()
    for copy in small:
        copy.wait()
    fill_table(rows, cols, table)
    table_copy.start()
    across = lax.broadcasted_iota(jnp.int32, (share, share), 1)
    along = lax.broadcasted_iota(jnp.int32, (share, share), 0)
    spread = jnp.sum(jnp.where(across == along, bias[...], 0.0), axis=1, keepdims=True)
    bias_all[mine, :] = jnp.broadcast_to(spread, (share, tile))
    for t in range(row_tiles):
        cot_load(t).wait()
    for d in range(1, n_help):
        cot_copy(d).start()
        bias_copy(d).start()
    weight_copy.wait()
    for h, place in ((0, turn_half[0]), (1, own_half)):
        w_t[:, pl.ds(pl.multiple_of(place * half, half), half)] = weight[h * half : (h + 1) * half, :].T
    wg[0] = jnp.zeros_like(wg.at[0])

    def pass_on(win, stage, turn, j):
        band_copy(win, stage, 0, turn, j).wait_recv()
        band_copy(win, stage, 1, turn, j).start()

    def settle(win, stage, turn):
        for j in range(chunks):
            band_copy(win, stage, 1, turn, j).wait_recv()
            core_copy(win, stage, 1, turn, j).start()
        for j in range(chunks):
            core_copy(win, stage, 0, turn, j).wait_recv()
            core_copy(win, stage, 1, turn, j).wait_recv()

    groups = slots // UNROLL
    marks = [i * groups // chunks for i in range(chunks + 1)]

    def aggregate(win, turn, between):
        def body(group, total):
            for u in range(UNROLL):
                t = group * UNROLL + u
                product = jnp.dot(tiles[meta[0, t]], win[turn][meta[1, t]], preferred_element_type=F32)
                total = total * meta[2, t].astype(F32) + product
                seg[turn, t] = total
            return total

        total = jnp.zeros((tile, half), F32)
        for i in range(chunks):
            total = lax.fori_loop(marks[i], marks[i + 1], body, total)
            between(i)

    def row_sum(turn, r):
        return seg[turn, meta[3, r]] * meta[4, r].astype(F32)

    def nothing(i):
        pass

    def send_part(h):
        for j in range(chunks):
            for r in range(j * per, (j + 1) * per):
                part[h, r] = row_sum(h, r).astype(BF16)
            for d in range(1, n_help):
                part_copy(h, j, d).start()

    for j in range(chunks):
        pass_on(win1, 0, 0, j)
    settle(win1, 0, 0)
    tile_copy.wait()
    table_copy.wait()
    aggregate(win1, 0, lambda i: pass_on(win1, 0, 1, i))
    send_part(0)
    for d in range(1, n_help):
        cot_copy(d).wait_recv()
        bias_copy(d).wait_recv()
    for t in range(row_tiles):
        cot[t] = cot_all[t].T
    bias_wide[...] = bias_all[...].T
    settle(win1, 0, 1)
    aggregate(win1, 1, nothing)
    send_part(1)

    for j in range(chunks):
        for h in range(HALVES):
            for d in range(1, n_help):
                part_copy(h, j, d).wait_recv()
        for r in range(j * per, (j + 1) * per):
            pieces = []
            for h in range(HALVES):
                total = row_sum(h, r)
                for d in range(1, n_help):
                    total = total + part_in[d - 1, h, r].astype(F32)
                pieces.append(total.astype(BF16))
            agg = jnp.concatenate(pieces, axis=1)
            pre = jnp.dot(agg, weight[...], preferred_element_type=F32) + bias_wide[...]
            ex = jnp.exp(jnp.minimum(pre, 0.0))
            grad = (cot[r].astype(F32) * ex).astype(BF16)
            back = jnp.dot(grad, w_t[...], preferred_element_type=F32).astype(BF16)
            for h in range(HALVES):
                win2[h][own_slot * row_tiles + r] = back[:, h * half : (h + 1) * half]
            out_all[r] = jnp.where(pre > 0.0, pre, ex - 1.0).astype(BF16).T
            gp_all[r] = grad.T
            held = gp_all[r, mine, :]
            wg[0, :, pl.ds(0, width)] += jnp.dot(held, agg, preferred_element_type=F32)
            wg[0, :, pl.ds(width, tile)] += held.astype(F32)
        band_copy(win2, 1, 0, 0, j).start()
        core_copy(win2, 1, 0, 0, j).start()
        if j > 0:
            pass_on(win2, 1, 0, j - 1)
    for j in range(chunks):
        band_copy(win2, 1, 0, 1, j).start()
        core_copy(win2, 1, 0, 1, j).start()
    pass_on(win2, 1, 0, chunks - 1)
    wg_copy(0).start()
    for t in range(row_tiles):
        out_ref[:, lanes(t)] = out_all[t, mine, :]

    def wg_turn(step):
        wg_copy(step).wait_recv()
        wg[step + 1] = wg[step] + wg_in[step]
        if step + 1 < steps:
            wg_copy(step + 1).start()

    def keep_sums(turn, early):
        for j in range(chunks):
            for r in range(j * per, (j + 1) * per):
                turned = row_sum(turn, r).T
                place = pl.ds(pl.multiple_of(turn_half[turn] * half, half), half)
                part2[r, place, :] = turned.astype(BF16)
                sums[r, place, :] = turned
            if early:
                for d in range(1, n_help):
                    back_copy(j, d).start()

    settle(win2, 1, 0)
    wg_turn(0)
    aggregate(win2, 0, lambda i: pass_on(win2, 1, 1, i))
    keep_sums(0, n_help == HALVES)
    wg_turn(1)
    settle(win2, 1, 1)
    aggregate(win2, 1, nothing)
    wg_turn(2)
    keep_sums(1, n_help != HALVES)
    for j in range(chunks):
        for d in range(1, n_help):
            back_copy(j, d).wait_recv()
        for r in range(j * per, (j + 1) * per):
            total = sums[r, mine, :]
            for d in range(1, n_help):
                total = total + part2_in[d - 1, r].astype(F32)
            prop_ref[:, lanes(r)] = total
    for s in range(3, steps):
        wg_turn(s)
    grads_ref[...] = wg[steps]

    for stage, win in ((0, win1), (1, win2)):
        for j in range(chunks):
            for kind in range(2):
                for turn in range(HALVES):
                    band_copy(win, stage, kind, turn, j).wait_send()
                    core_copy(win, stage, kind, turn, j).wait_send()
    for d in range(1, n_help):
        cot_copy(d).wait_send()
        bias_copy(d).wait_send()
        for j in range(chunks):
            for h in range(HALVES):
                part_copy(h, j, d).wait_send()
            back_copy(j, d).wait_send()
    for s in range(steps):
        wg_copy(s).wait_send()


def fill_table(rows, cols, table):
    slots = rows.shape[1]
    shape = (slots, slots)
    here = lax.broadcasted_iota(jnp.int32, shape, 0)
    there = lax.broadcasted_iota(jnp.int32, shape, 1)
    zero = jnp.zeros(shape, jnp.int32)
    one = zero + 1

    def upright(line):
        return jnp.sum(jnp.where(here == there, line, zero), axis=1, keepdims=True)

    def flat(mask, values):
        return jnp.sum(jnp.where(mask, values, zero), axis=0, keepdims=True)

    row_l = jnp.broadcast_to(rows[...], shape)
    row_s = jnp.broadcast_to(upright(row_l), shape)
    col_s = jnp.broadcast_to(upright(jnp.broadcast_to(cols[...], shape)), shape)
    before = row_l * slots + there < row_s * slots + here
    rank = jnp.broadcast_to(jnp.sum(jnp.where(before, one, zero), axis=1, keepdims=True), shape)
    placed = rank == there
    table[...] = jnp.zeros(table.shape, jnp.int32)
    table[0:1, 0:slots] = flat(placed, here)
    table[1:2, 0:slots] = flat(placed, col_s)
    goes_on = flat(placed, row_s) == flat(rank + 1 == there, row_s)
    table[2:3, 0:slots] = jnp.where(goes_on, 1, 0)
    table[3:4, 0:slots] = jnp.maximum(flat(row_s <= there, one) - 1, 0)
    table[4:5, 0:slots] = jnp.minimum(flat(row_s == there, one), 1)


def per_device(n_blk, n_help, features_t, weight, bias, cotangent_t, tile_vals, slot_row, slot_col):
    tiles = tile_vals[0, 0]
    slots, tile = tiles.shape[0], tiles.shape[-1]
    width, nodes = features_t.shape
    half = width // HALVES
    row_tiles = nodes // tile
    share = cotangent_t.shape[0]
    chunks = 4 if row_tiles % 4 == 0 else 1
    steps = n_blk.bit_length() - 1
    peers = n_help - 1
    vmem = pl.BlockSpec(memory_space=pltpu.VMEM)
    dma = pltpu.SemaphoreType.DMA
    output_t, propagated, grads = pl.pallas_call(
        functools.partial(layer_kernel, n_blk, n_help, chunks),
        out_shape=(
            jax.ShapeDtypeStruct((share, nodes), BF16),
            jax.ShapeDtypeStruct((share, nodes), F32),
            jax.ShapeDtypeStruct((share, width + tile), F32),
        ),
        in_specs=[pl.BlockSpec(memory_space=pltpu.HBM)] * 7,
        out_specs=(vmem, vmem, vmem),
        scratch_shapes=[
            pltpu.VMEM((1, slots), jnp.int32),
            pltpu.VMEM((1, slots), jnp.int32),
            pltpu.VMEM((1, share), F32),
            pltpu.VMEM((8, 128), jnp.int32),
            pltpu.SMEM((8, 128), jnp.int32),
            pltpu.VMEM((width, nodes), BF16),
            pltpu.VMEM((width, width), BF16),
            pltpu.VMEM((tile, width), F32),
            pltpu.VMEM((row_tiles, tile, width), BF16),
            *[pltpu.VMEM((SPANS * row_tiles, tile, half), BF16)] * (2 * HALVES),
            pltpu.VMEM((slots, tile, tile), BF16),
            pltpu.VMEM((HALVES, slots, tile, half), F32),
            pltpu.VMEM((HALVES, row_tiles, tile, half), BF16),
            pltpu.VMEM((peers, HALVES, row_tiles, tile, half), BF16),
            pltpu.VMEM((row_tiles, width, tile), BF16),
            pltpu.VMEM((peers, row_tiles, share, tile), BF16),
            pltpu.VMEM((width, tile), F32),
            pltpu.VMEM((row_tiles, width, tile), BF16),
            pltpu.VMEM((row_tiles, width, tile), BF16),
            pltpu.VMEM((row_tiles, width, tile), BF16),
            pltpu.VMEM((width, width), BF16),
            pltpu.VMEM((steps + 1, share, width + tile), F32),
            pltpu.VMEM((steps, share, width + tile), F32),
            pltpu.VMEM((row_tiles, width, tile), F32),
            dma((4,)),
            dma((HALVES, chunks)),
            dma,
            dma,
            dma((row_tiles,)),
            dma((2, 2, HALVES, chunks)),
            dma((2, 2, HALVES, chunks)),
            dma((2, 2, HALVES, chunks)),
            dma((2, 2, HALVES, chunks)),
            dma((HALVES, chunks, peers)),
            dma((HALVES, chunks, peers)),
            dma((2, peers)),
            dma((2, peers)),
            dma((chunks, peers)),
            dma((chunks, peers)),
            dma((steps,)),
            dma((steps,)),
        ],
        compiler_params=pltpu.CompilerParams(
            collective_id=0, has_side_effects=True, vmem_limit_bytes=VMEM_MIB * 1024 * 1024
        ),
    )(slot_row[0], slot_col[0], features_t, weight, bias.reshape(1, share), cotangent_t, tiles)
    scale = 1.0 / math.sqrt(nodes * n_blk)
    weight_grad = grads[:, :width].T * scale
    bias_grad = jnp.sum(grads[:, width:], axis=1) * scale
    return (output_t, propagated, weight_grad, bias_grad)


def solution(mesh):
    placed = (
        P(None, "blk"),
        P(),
        P("help"),
        P("help", "blk"),
        P("blk", "help", None, None, None),
        P("blk", "help", None),
        P("blk", "help", None),
    )
    return jax.shard_map(
        functools.partial(per_device, mesh.shape["blk"], mesh.shape["help"]),
        mesh=mesh,
        in_specs=placed,
        out_specs=(P("help", "blk"), P("help", "blk"), P(None, "help"), P("help")),
        check_vma=False,
    )
```

time: 102 us -> 93.1 us (0.913)
  Pallas kernels: 89 us -> 85.2 us
  other arithmetic: 4.99 us -> 2.38 us
  local copies, waits for them, and re-layouts: 6.59 us -> 4.59 us
    pallas_call x1, Pallas kernels: 89 us -> 85.2 us  [per_device(): pl.pallas_call(functools.partial(layer_kernel, n_blk, n_help, chunks), ou...]
    broadcast_in_dim x1 -> x0, local copies, waits for them, and re-layouts: 1.37 us -> none  [per_device(): bias_wide = jnp.broadcast_to(bias[:, None], (share, tile))]
where the time goes in v3:
time: 93.1 us; the launch traced here: 92.9 us
  Pallas kernels  85.2 us (92%)
  local copies, waits for them, and re-layouts  4.59 us (5%)
  other arithmetic  2.38 us (3%)
    pallas_call x1, Pallas kernels, per_device(): pl.pallas_call(functools.partial(layer_kernel, n_blk, n_help, chunks), ou...  85.2 us
    unnamed x3, local copies, waits for them, and re-layouts  4.59 us

profile of v3, /device:TPU:0, one launch (start us, length us, event | category | flops | bytes accessed | tf_op | source)
XLA Modules:
  0.0 92.9 jit_solution(16826539539551517428)
XLA Ops:
  0.6 85.2 %shard_map.102 = (bf16[128,1536]{1,0:T(8,128)(2,1)}, f32[128,1536]{1,0:T(8,128)}, f32[128,384]{1,0:T(8,128)}) custom-call(s32[1,80]{1,0:T(1,128)} %bitcast.7, s32[1,80]{1,0:T(1,128)} %bitcast.8, bf16[256,1536]{1,0:T(8,128)(2,1)} %feat_hbm.1, bf16[256,256]{1,0:T(8,128)(2,1)} %weight_hbm.1, f32[1,128]{1,0:T(1,128)} %bitcast.9, bf16[128,1536]{1,0:T(8,128)(2,1)} %cot_hbm.1, ...), custom_call_target="tpu_custom_call" | custom-call | tf_op jit(solution)/shard_map/pallas_call | solution.py:381
  85.9 0.9 %slice_reduce_fusion = f32[128]{0:T(128)S(1)} fusion(f32[128,384]{1,0:T(8,128)} %get-tuple-element.9), kind=kLoop, calls=%fused_computation.1 | loop fusion | flops 16256 | bytes 66048 | tf_op jit(solution)/shard_map/reduce_sum | solution.py:439
  86.8 0.9 multiply_bitcast_fusion
  87.8 0.8 copy.11
  88.5 0.5 broadcast_multiply_fusion
  89.0 1.8 %copy.14 = bf16[128,1536]{1,0:T(8,128)(2,1)} copy(bf16[128,1536]{1,0:T(8,128)(2,1)} %get-tuple-element.18) | data formatting | bytes 786432
  90.8 2.1 %copy.15 = f32[128,1536]{1,0:T(8,128)} copy(f32[128,1536]{1,0:T(8,128)} %get-tuple-element.19) | data formatting | bytes 1572864

commit v4 on v3

--- a/solution.py
+++ b/solution.py
@@ -12,6 +12,7 @@
 SPANS = 2 * BAND + 1
 UNROLL = 8
 HALVES = 2
+AHEAD = 2
 VMEM_MIB = 60
 MESH = pl.DeviceIdType.MESH
 F32 = jnp.float32
@@ -154,6 +155,18 @@
             device_id={"blk": flip(step)}, device_id_type=MESH,
         )
 
+    def launch(win, stage, k):
+        band_copy(win, stage, 0, k // chunks, k % chunks).start()
+        core_copy(win, stage, 0, k // chunks, k % chunks).start()
+
+    def pass_on(win, stage, k, more=True):
+        turn, j = k // chunks, k % chunks
+        band_copy(win, stage, 0, turn, j).wait_recv()
+        band_copy(win, stage, 1, turn, j).start()
+        band_copy(win, stage, 0, turn, j).wait_send()
+        if more and k + AHEAD < HALVES * chunks:
+            launch(win, stage, k + AHEAD)
+
     for copy in small:
         copy.start()
     weight_copy.start()
@@ -167,9 +180,8 @@
                 win1[h][own_slot * row_tiles + t] = feat[h * half : (h + 1) * half, lanes(t)].T
             if h == 0 and j == 0:
                 pl.semaphore_wait(barrier, len(peers) + n_help - 1)
-            band_copy(win1, 0, 0, h, j).start()
-        for j in range(chunks):
-            core_copy(win1, 0, 0, h, j).start()
+            if h * chunks + j < AHEAD:
+                launch(win1, 0, h * chunks + j)
     for copy in small:
         copy.wait()
     fill_table(rows, cols, table)
@@ -188,10 +200,6 @@
         w_t[:, pl.ds(pl.multiple_of(place * half, half), half)] = weight[h * half : (h + 1) * half, :].T
     wg[0] = jnp.zeros_like(wg.at[0])
 
-    def pass_on(win, stage, turn, j):
-        band_copy(win, stage, 0, turn, j).wait_recv()
-        band_copy(win, stage, 1, turn, j).start()
-
     def settle(win, stage, turn):
         for j in range(chunks):
             band_copy(win, stage, 1, turn, j).wait_recv()
@@ -227,15 +235,16 @@
         for j in range(chunks):
             for r in range(j * per, (j + 1) * per):
                 part[h, r] = row_sum(h, r).astype(BF16)
-            for d in range(1, n_help):
-                part_copy(h, j, d).start()
+            if h == 0 or j < AHEAD:
+                for d in range(1, n_help):
+                    part_copy(h, j, d).start()
 
     for j in range(chunks):
-        pass_on(win1, 0, 0, j)
+        pass_on(win1, 0, j)
     settle(win1, 0, 0)
     tile_copy.wait()
     table_copy.wait()
-    aggregate(win1, 0, lambda i: pass_on(win1, 0, 1, i))
+    aggregate(win1, 0, lambda i: pass_on(win1, 0, chunks + i))
     send_part(0)
     for d in range(1, n_help):
         cot_copy(d).wait_recv()
@@ -251,6 +260,10 @@
         for h in range(HALVES):
             for d in range(1, n_help):
                 part_copy(h, j, d).wait_recv()
+        for d in range(1, n_help):
+            part_copy(1, j, d).wait_send()
+            if j + AHEAD < chunks:
+                part_copy(1, j + AHEAD, d).start()
         for r in range(j * per, (j + 1) * per):
             pieces = []
             for h in range(HALVES):
@@ -270,14 +283,11 @@
             held = gp_all[r, mine, :]
             wg[0, :, pl.ds(0, width)] += jnp.dot(held, agg, preferred_element_type=F32)
             wg[0, :, pl.ds(width, tile)] += held.astype(F32)
-        band_copy(win2, 1, 0, 0, j).start()
-        core_copy(win2, 1, 0, 0, j).start()
+        launch(win2, 1, j)
         if j > 0:
-            pass_on(win2, 1, 0, j - 1)
-    for j in range(chunks):
-        band_copy(win2, 1, 0, 1, j).start()
-        core_copy(win2, 1, 0, 1, j).start()
-    pass_on(win2, 1, 0, chunks - 1)
+            pass_on(win2, 1, j - 1, False)
+    launch(win2, 1, chunks)
+    pass_on(win2, 1, chunks - 1)
     wg_copy(0).start()
     for t in range(row_tiles):
         out_ref[:, lanes(t)] = out_all[t, mine, :]
@@ -301,7 +311,7 @@
 
     settle(win2, 1, 0)
     wg_turn(0)
-    aggregate(win2, 0, lambda i: pass_on(win2, 1, 1, i))
+    aggregate(win2, 0, lambda i: pass_on(win2, 1, chunks + i))
     keep_sums(0, n_help == HALVES)
     wg_turn(1)
     settle(win2, 1, 1)
@@ -322,16 +332,15 @@
 
     for stage, win in ((0, win1), (1, win2)):
         for j in range(chunks):
-            for kind in range(2):
-                for turn in range(HALVES):
-                    band_copy(win, stage, kind, turn, j).wait_send()
+            for turn in range(HALVES):
+                band_copy(win, stage, 1, turn, j).wait_send()
+                for kind in range(2):
                     core_copy(win, stage, kind, turn, j).wait_send()
     for d in range(1, n_help):
         cot_copy(d).wait_send()
         bias_copy(d).wait_send()
         for j in range(chunks):
-            for h in range(HALVES):
-                part_copy(h, j, d).wait_send()
+            part_copy(0, j, d).wait_send()
             back_copy(j, d).wait_send()
     for s in range(steps):
         wg_copy(s).wait_send()
@@ -364,6 +373,22 @@
     table[2:3, 0:slots] = jnp.where(goes_on, 1, 0)
     table[3:4, 0:slots] = jnp.maximum(flat(row_s <= there, one) - 1, 0)
     table[4:5, 0:slots] = jnp.minimum(flat(row_s == there, one), 1)
+
+
+def finish_kernel(pieces, scale, out_in, prop_in, grads, out_ref, prop_ref, weight_grad, bias_grad, out_sem, prop_sem):
+    rows = out_in.shape[0] // pieces
+    width = weight_grad.shape[0]
+    copies = []
+    for i in range(pieces):
+        part = pl.ds(i * rows, rows)
+        copies.append(pltpu.make_async_copy(out_in.at[part], out_ref.at[part], out_sem.at[i]))
+        copies.append(pltpu.make_async_copy(prop_in.at[part], prop_ref.at[part], prop_sem.at[i]))
+    for copy in copies:
+        copy.start()
+    weight_grad[...] = grads[:, 0:width].T * scale
+    bias_grad[...] = jnp.sum(grads[:, width:].T, axis=0, keepdims=True) * scale
+    for copy in copies:
+        copy.wait()
 
 
 def per_device(n_blk, n_help, features_t, weight, bias, cotangent_t, tile_vals, slot_row, slot_col):
@@ -435,9 +460,22 @@
         ),
     )(slot_row[0], slot_col[0], features_t, weight, bias.reshape(1, share), cotangent_t, tiles)
     scale = 1.0 / math.sqrt(nodes * n_blk)
-    weight_grad = grads[:, :width].T * scale
-    bias_grad = jnp.sum(grads[:, width:], axis=1) * scale
-    return (output_t, propagated, weight_grad, bias_grad)
+    anywhere = pl.BlockSpec(memory_space=pltpu.HBM)
+    pieces = 4 if share % 64 == 0 else 2
+    output_t, propagated, weight_grad, bias_grad = pl.pallas_call(
+        functools.partial(finish_kernel, pieces, scale),
+        out_shape=(
+            jax.ShapeDtypeStruct((share, nodes), BF16),
+            jax.ShapeDtypeStruct((share, nodes), F32),
+            jax.ShapeDtypeStruct((width, share), F32),
+            jax.ShapeDtypeStruct((1, share), F32),
+        ),
+        in_specs=[anywhere, anywhere, vmem],
+        out_specs=(anywhere, anywhere, vmem, vmem),
+        scratch_shapes=[dma((pieces,)), dma((pieces,))],
+        compiler_params=pltpu.CompilerParams(vmem_limit_bytes=VMEM_MIB * 1024 * 1024),
+    )(output_t, propagated, grads)
+    return (output_t, propagated, weight_grad, bias_grad.reshape(share))
 
 
 def solution(mesh):

time: 93.1 us -> 129 us (1.39)
  Pallas kernels: 85.2 us -> 128 us
  local copies, waits for them, and re-layouts: 4.59 us -> 0 us
  other arithmetic: 2.38 us -> 0 us
    pallas_call x0 -> x1, Pallas kernels: none -> 38.5 us  [per_device(): pl.pallas_call(functools.partial(finish_kernel, pieces, scale), out_shape...]
    unnamed x3 -> x0, local copies, waits for them, and re-layouts: 4.59 us -> none
    pallas_call x1, Pallas kernels: 85.2 us -> 89.7 us  [per_device(): pl.pallas_call(functools.partial(layer_kernel, n_blk, n_help, chunks), ou...]
    mul x2 -> x0, other arithmetic: 1.44 us -> none  [the longest x1 0.93 us: per_device(): weight_grad = grads[:, :width].T * scale]
where the time goes in v4:
time: 129 us
  Pallas kernels  128 us (99%)
    pallas_call x1, Pallas kernels, per_device(): pl.pallas_call(functools.partial(layer_kernel, n_blk, n_help, chunks), ou...  89.7 us
    pallas_call x1, Pallas kernels, per_device(): pl.pallas_call(functools.partial(finish_kernel, pieces, scale), out_shape...  38.5 us

profile of v4, /device:TPU:0, one launch (start us, length us, event | category | flops | bytes accessed | tf_op | source)
XLA Modules:
  0.0 128.8 jit_solution(1008599622847027655)
XLA Ops:
  0.6 89.7 %shard_map.102 = (bf16[128,1536]{1,0:T(8,128)(2,1)}, f32[128,1536]{1,0:T(8,128)}, f32[128,384]{1,0:T(8,128)}) custom-call(s32[1,80]{1,0:T(1,128)} %bitcast.6, s32[1,80]{1,0:T(1,128)} %bitcast.7, bf16[256,1536]{1,0:T(8,128)(2,1)} %feat_hbm.1, bf16[256,256]{1,0:T(8,128)(2,1)} %weight_hbm.1, f32[1,128]{1,0:T(1,128)} %bitcast.8, bf16[128,1536]{1,0:T(8,128)(2,1)} %cot_hbm.1, ...), custom_call_target="tpu_custom_call" | custom-call | tf_op jit(solution)/shard_map/pallas_call | solution.py:406
  90.3 38.5 %shard_map.103 = (bf16[128,1536]{1,0:T(8,128)(2,1)}, f32[128,1536]{1,0:T(8,128)}, f32[256,128]{1,0:T(8,128)}, f32[1,128]{1,0:T(1,128)}) custom-call(bf16[128,1536]{1,0:T(8,128)(2,1)} %get-tuple-element.11.out_in, f32[128,1536]{1,0:T(8,128)} %get-tuple-element.12.prop_in, f32[128,384]{1,0:T(8,128)} %get-tuple-element.13.grads), custom_call_target="tpu_custom_call" | custom-call | tf_op jit(solution)/shard_map/pallas_call | solution.py:465

commit v5 on v3

--- a/solution.py
+++ b/solution.py
@@ -10,7 +10,8 @@
 
 BAND = 2
 SPANS = 2 * BAND + 1
-UNROLL = 8
+UNROLL = 4
+QUAD = 4
 HALVES = 2
 VMEM_MIB = 60
 MESH = pl.DeviceIdType.MESH
@@ -31,7 +32,7 @@
     blk = lax.axis_index("blk")
     helper = lax.axis_index("help")
     row_tiles = feat.shape[1] // tiles.shape[-1]
-    slots = tiles.shape[0]
+    slots = tiles_hbm.shape[0]
     tile = tiles.shape[-1]
     width = weight.shape[0]
     half = width // HALVES
@@ -90,7 +91,7 @@
         pltpu.make_async_copy(bias_hbm, bias, small_sem.at[2]),
     ]
     table_copy = pltpu.make_async_copy(table, meta, small_sem.at[3])
-    tile_copy = pltpu.make_async_copy(tiles_hbm, tiles, tile_sem)
+    tile_copy = pltpu.make_async_copy(tiles_hbm, tiles.at[pl.ds(0, slots)], tile_sem)
     weight_copy = pltpu.make_async_copy(weight_hbm, weight, weight_sem)
 
     def span(slot, j):
@@ -172,7 +173,8 @@
             core_copy(win1, 0, 0, h, j).start()
     for copy in small:
         copy.wait()
-    fill_table(rows, cols, table)
+    tiles[slots] = jnp.zeros((tile, tile), BF16)
+    fill_table(rows, cols, table, row_tiles)
     table_copy.start()
     across = lax.broadcasted_iota(jnp.int32, (share, share), 1)
     along = lax.broadcasted_iota(jnp.int32, (share, share), 0)
@@ -200,15 +202,17 @@
             core_copy(win, stage, 0, turn, j).wait_recv()
             core_copy(win, stage, 1, turn, j).wait_recv()
 
-    groups = slots // UNROLL
+    groups = seg.shape[1] // UNROLL
     marks = [i * groups // chunks for i in range(chunks + 1)]
 
     def aggregate(win, turn, between):
         def body(group, total):
             for u in range(UNROLL):
                 t = group * UNROLL + u
-                product = jnp.dot(tiles[meta[0, t]], win[turn][meta[1, t]], preferred_element_type=F32)
-                total = total * meta[2, t].astype(F32) + product
+                left = jnp.concatenate([tiles[meta[0, t * QUAD + i]] for i in range(QUAD)], axis=1)
+                right = jnp.concatenate([win[turn][meta[1, t * QUAD + i]] for i in range(QUAD)], axis=0)
+                product = jnp.dot(left, right, preferred_element_type=F32)
+                total = total * meta[2, t * QUAD].astype(F32) + product
                 seg[turn, t] = total
             return total
 
@@ -337,33 +341,55 @@
         wg_copy(s).wait_send()
 
 
-def fill_table(rows, cols, table):
+def fill_table(rows, cols, table, row_tiles):
     slots = rows.shape[1]
+    places = table.shape[1]
     shape = (slots, slots)
+    wide = (slots, places)
     here = lax.broadcasted_iota(jnp.int32, shape, 0)
     there = lax.broadcasted_iota(jnp.int32, shape, 1)
     zero = jnp.zeros(shape, jnp.int32)
     one = zero + 1
-
-    def upright(line):
-        return jnp.sum(jnp.where(here == there, line, zero), axis=1, keepdims=True)
+    place = lax.broadcasted_iota(jnp.int32, wide, 1)
+    slot = lax.broadcasted_iota(jnp.int32, wide, 0)
+    none = jnp.zeros(wide, jnp.int32)
+
+    def upright(mask, values):
+        return jnp.sum(jnp.where(mask, values, zero), axis=1, keepdims=True)
 
     def flat(mask, values):
         return jnp.sum(jnp.where(mask, values, zero), axis=0, keepdims=True)
 
+    def flat_wide(mask, values):
+        return jnp.sum(jnp.where(mask, values, none), axis=0, keepdims=True)
+
     row_l = jnp.broadcast_to(rows[...], shape)
-    row_s = jnp.broadcast_to(upright(row_l), shape)
-    col_s = jnp.broadcast_to(upright(jnp.broadcast_to(cols[...], shape)), shape)
-    before = row_l * slots + there < row_s * slots + here
-    rank = jnp.broadcast_to(jnp.sum(jnp.where(before, one, zero), axis=1, keepdims=True), shape)
-    placed = rank == there
+    row_u = upright(here == there, row_l)
+    row_s = jnp.broadcast_to(row_u, shape)
+    row_w = jnp.broadcast_to(row_u, wide)
+    col_w = jnp.broadcast_to(upright(here == there, jnp.broadcast_to(cols[...], shape)), wide)
+    count = flat(row_s == there, one)
+    filled = jnp.broadcast_to(jnp.bitwise_and(count + (QUAD - 1), -QUAD), shape)
+    head = upright((row_l == row_s) & (there < here), one)
+    start = upright(there < row_s, filled)
+    spot = jnp.where(row_w < row_tiles, jnp.broadcast_to(start + head, wide), none - 2 * QUAD)
+    filled_s = jnp.broadcast_to(upright(here == there, filled), shape)
+    placed = spot == place
     table[...] = jnp.zeros(table.shape, jnp.int32)
-    table[0:1, 0:slots] = flat(placed, here)
-    table[1:2, 0:slots] = flat(placed, col_s)
-    goes_on = flat(placed, row_s) == flat(rank + 1 == there, row_s)
-    table[2:3, 0:slots] = jnp.where(goes_on, 1, 0)
-    table[3:4, 0:slots] = jnp.maximum(flat(row_s <= there, one) - 1, 0)
-    table[4:5, 0:slots] = jnp.minimum(flat(row_s == there, one), 1)
+    table[0:1, :] = flat_wide(placed, slot - slots) + slots
+    table[1:2, :] = flat_wide(placed, col_w)
+    goes_on = flat_wide(placed, row_w) == flat_wide(spot + QUAD == place, row_w)
+    table[2:3, :] = jnp.where(goes_on, 1, 0)
+    table[3:4, 0:slots] = jnp.maximum(jnp.right_shift(flat(here <= there, filled_s), 2) - 1, 0)
+    table[4:5, 0:slots] = jnp.minimum(count, 1)
+
+
+def finish_kernel(scale, out_in, prop_in, grads, out_ref, prop_ref, weight_grad, bias_grad):
+    width = weight_grad.shape[0]
+    out_ref[...] = out_in[...]
+    prop_ref[...] = prop_in[...]
+    weight_grad[...] = grads[:, 0:width].T * scale
+    bias_grad[...] = jnp.sum(grads[:, width:].T, axis=0, keepdims=True) * scale
 
 
 def per_device(n_blk, n_help, features_t, weight, bias, cotangent_t, tile_vals, slot_row, slot_col):
@@ -374,6 +400,7 @@
     row_tiles = nodes // tile
     share = cotangent_t.shape[0]
     chunks = 4 if row_tiles % 4 == 0 else 1
+    quads = -(-(slots + row_tiles * (QUAD - 1)) // (QUAD * UNROLL * chunks)) * UNROLL * chunks
     steps = n_blk.bit_length() - 1
     peers = n_help - 1
     vmem = pl.BlockSpec(memory_space=pltpu.VMEM)
@@ -398,8 +425,8 @@
             pltpu.VMEM((tile, width), F32),
             pltpu.VMEM((row_tiles, tile, width), BF16),
             *[pltpu.VMEM((SPANS * row_tiles, tile, half), BF16)] * (2 * HALVES),
-            pltpu.VMEM((slots, tile, tile), BF16),
-            pltpu.VMEM((HALVES, slots, tile, half), F32),
+            pltpu.VMEM((slots + 1, tile, tile), BF16),
+            pltpu.VMEM((HALVES, quads, tile, half), F32),
             pltpu.VMEM((HALVES, row_tiles, tile, half), BF16),
             pltpu.VMEM((peers, HALVES, row_tiles, tile, half), BF16),
             pltpu.VMEM((row_tiles, width, tile), BF16),
@@ -435,9 +462,19 @@
         ),
     )(slot_row[0], slot_col[0], features_t, weight, bias.reshape(1, share), cotangent_t, tiles)
     scale = 1.0 / math.sqrt(nodes * n_blk)
-    weight_grad = grads[:, :width].T * scale
-    bias_grad = jnp.sum(grads[:, width:], axis=1) * scale
-    return (output_t, propagated, weight_grad, bias_grad)
+    output_t, propagated, weight_grad, bias_grad = pl.pallas_call(
+        functools.partial(finish_kernel, scale),
+        out_shape=(
+            jax.ShapeDtypeStruct((share, nodes), BF16),
+            jax.ShapeDtypeStruct((share, nodes), F32),
+            jax.ShapeDtypeStruct((width, share), F32),
+            jax.ShapeDtypeStruct((1, share), F32),
+        ),
+        in_specs=[vmem] * 3,
+        out_specs=(vmem,) * 4,
+        compiler_params=pltpu.CompilerParams(vmem_limit_bytes=VMEM_MIB * 1024 * 1024),
+    )(output_t, propagated, grads)
+    return (output_t, propagated, weight_grad, bias_grad.reshape(share))
 
 
 def solution(mesh):

time: 93.1 us -> 88.9 us (0.955)
  local copies, waits for them, and re-layouts: 4.59 us -> 0 us
  Pallas kernels: 85.2 us -> 88.1 us
  other arithmetic: 2.38 us -> 0 us
    unnamed x3 -> x0, local copies, waits for them, and re-layouts: 4.59 us -> none
    pallas_call x0 -> x1, Pallas kernels: none -> 2.41 us  [per_device(): pl.pallas_call(functools.partial(finish_kernel, scale), out_shape=(jax.Sh...]
    mul x2 -> x0, other arithmetic: 1.44 us -> none  [the longest x1 0.93 us: per_device(): weight_grad = grads[:, :width].T * scale]
    reduce_sum x1 -> x0, other arithmetic: 0.94 us -> none  [per_device(): bias_grad = jnp.sum(grads[:, width:], axis=1) * scale]
where the time goes in v5:
time: 88.9 us; the launch traced here: 88.8 us
  Pallas kernels  88.1 us (99%)
    pallas_call x1, Pallas kernels, per_device(): pl.pallas_call(functools.partial(layer_kernel, n_blk, n_help, chunks), ou...  85.7 us
    pallas_call x1, Pallas kernels, per_device(): pl.pallas_call(functools.partial(finish_kernel, scale), out_shape=(jax.Sh...  2.41 us

profile of v5, /device:TPU:0, one launch (start us, length us, event | category | flops | bytes accessed | tf_op | source)
XLA Modules:
  0.0 88.8 jit_solution(12133768037253427291)
XLA Ops:
  0.6 85.7 %shard_map.102 = (bf16[128,1536]{1,0:T(8,128)(2,1)}, f32[128,1536]{1,0:T(8,128)}, f32[128,384]{1,0:T(8,128)}) custom-call(s32[1,80]{1,0:T(1,128)} %bitcast.6, s32[1,80]{1,0:T(1,128)} %bitcast.7, bf16[256,1536]{1,0:T(8,128)(2,1)} %feat_hbm.1, bf16[256,256]{1,0:T(8,128)(2,1)} %weight_hbm.1, f32[1,128]{1,0:T(1,128)} %bitcast.8, bf16[128,1536]{1,0:T(8,128)(2,1)} %cot_hbm.1, ...), custom_call_target="tpu_custom_call" | custom-call | tf_op jit(solution)/shard_map/pallas_call | solution.py:408
  86.4 2.4 %shard_map.103 = (bf16[128,1536]{1,0:T(8,128)(2,1)}, f32[128,1536]{1,0:T(8,128)}, f32[256,128]{1,0:T(8,128)}, f32[1,128]{1,0:T(1,128)}) custom-call(bf16[128,1536]{1,0:T(8,128)(2,1)} %get-tuple-element.11.out_in, f32[128,1536]{1,0:T(8,128)} %get-tuple-element.12.prop_in, f32[128,384]{1,0:T(8,128)} %get-tuple-element.13.grads), custom_call_target="tpu_custom_call" | custom-call | tf_op jit(solution)/shard_map/pallas_call | solution.py:465
